TPU v7x, 256 devices: a whole 4x4x8 slice. The times are simulated.
256 devices in a mesh: dp: 4 (over x), seq: 64 (over y, z, core).
Axes of the slice: x: 4, y: 4, z: 8, core: 2. Of those that a mesh axis runs over, the one named last changes fastest.
Arguments:
- spatial_qkv: bfloat16 [3, 32768, 1536], P(None, ('dp', 'seq')), parts along dimension 1, may hold values from -6 to 6
- temporal_qkv: bfloat16 [3, 32768, 1536], P(None, ('dp', 'seq')), parts along dimension 1, may hold values from -6 to 6
- cross_query: bfloat16 [32768, 1536], P(('dp', 'seq')), parts along dimension 0, may hold values from -6 to 6
- caption_kv: bfloat16 [1280, 2, 1536], P(('dp', 'seq')), parts along dimension 0, may hold values from -6 to 6
- out_grad: bfloat16 [32768, 1536], P(('dp', 'seq')), parts along dimension 0, may hold values from -6 to 6
- live_tokens: int32 [4], P('dp'), parts along dimension 0, may hold values from 2048 to 8192, as said below
- caption_len: int32 [4], P('dp'), parts along dimension 0, may hold values from 80 to 320, as said below
Outputs:
- mixed: bfloat16 [32768, 1536], P(('dp', 'seq')), parts along dimension 0
- spatial_grads: bfloat16 [3, 32768, 1536], P(None, ('dp', 'seq')), parts along dimension 1
- temporal_grads: bfloat16 [3, 32768, 1536], P(None, ('dp', 'seq')), parts along dimension 1
- cross_query_grad: bfloat16 [32768, 1536], P(('dp', 'seq')), parts along dimension 0
- caption_grads: float32 [1280, 2, 1536], P(('dp', 'seq')), parts along dimension 0
There are 4 independent parts, one for each index of `dp`. A program takes and returns all parts, laid end to end along the dimension named above; each array names one. Nothing has to cross between parts.
Inputs may be any that keep to these rules, and one draw needn't show every extreme that they name: Tokens from live_tokens on are padding. Caption rows from caption_len on are padding.
All inputs are finite; a program needn't handle non-finite values.
Results may differ from a plain program's by a relative error of at most 0.035.
Values may be sent and summed in bfloat16 or wider, within the bound.
No kernel may reach another device: no remote copies, remote signals or barrier semaphores. Data moves between devices by JAX's collectives and lax.ppermute only.
A program may use at most 128 MiB of HBM per device.

v0:
```python
import jax
import jax.numpy as jnp
from jax import lax
from jax.sharding import PartitionSpec as P

HDIM = 128
P_SIZE = 512


def swapped(shard, axis, apart):
    return lax.ppermute(shard, axis, [(i, i ^ 1 << apart) for i in range(lax.axis_size(axis))])


def score_rows(queries, key_rows, key_keep):
    scale_factor = queries.shape[-1] ** (-0.5)
    scores = (
        jnp.einsum("bnhe,bmhe->bhnm", queries, key_rows, preferred_element_type=jnp.float32)
        * scale_factor
    )
    return jnp.where(key_keep, scores, -1e30)


def weight_rows(scores, largest, denominator):
    weights = jnp.exp(scores - largest[..., None]) / denominator[..., None]
    return (weights, weights.astype(jnp.bfloat16))


def slope_rows(weights, grad_rows, value_rows, row_delta):
    dprobs = jnp.einsum(
        "bnhe,bmhe->bhnm", grad_rows, value_rows, preferred_element_type=jnp.float32
    )
    return (weights * (dprobs - row_delta[..., None])).astype(jnp.bfloat16)


def attend_forward(queries, key_rows, value_rows, grad_rows, key_keep):
    scale_factor = queries.shape[-1] ** (-0.5)
    scores = score_rows(queries, key_rows, key_keep)
    largest = jnp.max(scores, axis=-1)
    denominator = jnp.sum(jnp.exp(scores - largest[..., None]), axis=-1)
    weights, weights_low = weight_rows(scores, largest, denominator)
    branch = jnp.einsum(
        "bhnm,bmhe->bnhe", weights_low, value_rows, preferred_element_type=jnp.float32
    ).astype(jnp.bfloat16)
    row_delta = jnp.einsum("bnhe,bnhe->bhn", grad_rows, branch, preferred_element_type=jnp.float32)
    dscores = slope_rows(weights, grad_rows, value_rows, row_delta)
    query_grad = (
        jnp.einsum("bhnm,bmhe->bnhe", dscores, key_rows, preferred_element_type=jnp.float32)
        * scale_factor
    )
    return (branch, query_grad, weights_low, dscores, largest, denominator, row_delta)


def key_terms(queries, grad_rows, weights_low, dscores):
    scale_factor = queries.shape[-1] ** (-0.5)
    key_grad = (
        jnp.einsum("bhnm,bnhe->bmhe", dscores, queries, preferred_element_type=jnp.float32)
        * scale_factor
    )
    value_grad = jnp.einsum(
        "bhnm,bnhe->bmhe", weights_low, grad_rows, preferred_element_type=jnp.float32
    )
    return (key_grad, value_grad)


def ordered(low_half, mine, theirs, axis_number):
    return jnp.where(
        low_half,
        jnp.concatenate([mine, theirs], axis=axis_number),
        jnp.concatenate([theirs, mine], axis=axis_number),
    )


def local(spatial_qkv, temporal_qkv, cross_query, caption_kv, out_grad, live_tokens, caption_len):
    devices = lax.axis_size("seq")
    dev_index = lax.axis_index("seq")
    tok_rows = out_grad.shape[0]
    feature_width = out_grad.shape[1]
    head_count = feature_width // HDIM
    token_ids = dev_index * tok_rows + jnp.arange(tok_rows)
    live_rows = token_ids < live_tokens[0]
    grad_rows = jnp.where(live_rows[:, None], out_grad, jnp.zeros_like(out_grad))

    def split_heads(tensor, batch_count):
        return tensor.reshape(batch_count, -1, head_count, HDIM)

    def join_heads(tensor):
        return tensor.reshape(tok_rows, feature_width)

    group_bits = (P_SIZE // tok_rows).bit_length() - 1
    every_key = jnp.ones((P_SIZE,), jnp.bool_)
    frame_kv = spatial_qkv[1:3]
    for bit_number in range(group_bits):
        partner = swapped(frame_kv, "seq", bit_number)
        low_half = dev_index // 2**bit_number % 2 == 0
        frame_kv = ordered(low_half, frame_kv, partner, 1)
    own_queries = split_heads(spatial_qkv[0], 1)
    own_grad = split_heads(grad_rows, 1)
    results = attend_forward(
        own_queries, split_heads(frame_kv[0], 1), split_heads(frame_kv[1], 1), own_grad, every_key
    )
    spatial_out, spatial_dq = (results[0], results[1])
    key_part, value_part = key_terms(own_queries, own_grad, results[2], results[3])
    grad_sums = jnp.stack(
        [key_part.reshape(P_SIZE, feature_width), value_part.reshape(P_SIZE, feature_width)]
    )
    for bit_number in reversed(range(group_bits)):
        half_rows = grad_sums.shape[1] // 2
        up_half = dev_index // 2**bit_number % 2
        kept_half = lax.dynamic_slice_in_dim(grad_sums, up_half * half_rows, half_rows, 1)
        sent_half = lax.dynamic_slice_in_dim(grad_sums, (1 - up_half) * half_rows, half_rows, 1)
        grad_sums = kept_half + swapped(sent_half.astype(jnp.bfloat16), "seq", bit_number).astype(
            sent_half.dtype
        )
    key_grad, value_grad = (grad_sums[0], grad_sums[1])
    spatial_grads = jnp.stack(
        [join_heads(spatial_dq), join_heads(key_grad), join_heads(value_grad)]
    ).astype(jnp.bfloat16)
    piece_rows = tok_rows // devices

    def pixel_split(tensor):
        return tensor.reshape(piece_rows, devices, head_count, HDIM)

    parts = (
        lax.all_to_all(
            pixel_split(temporal_qkv[0]), "seq", split_axis=1, concat_axis=0, tiled=True
        ),
        lax.all_to_all(
            pixel_split(temporal_qkv[1]), "seq", split_axis=1, concat_axis=0, tiled=True
        ),
        lax.all_to_all(
            pixel_split(temporal_qkv[2]), "seq", split_axis=1, concat_axis=0, tiled=True
        ),
        lax.all_to_all(pixel_split(grad_rows), "seq", split_axis=1, concat_axis=0, tiled=True),
    )
    pixels_here = P_SIZE // devices
    frame_total = tok_rows // pixels_here
    item_heads = parts[0].shape[2]

    def by_pixel(tensor):
        return jnp.swapaxes(tensor.reshape(frame_total, pixels_here, item_heads, HDIM), 0, 1)

    def back_rows(tensor):
        return jnp.swapaxes(tensor, 0, 1).reshape(tok_rows, 1, item_heads, HDIM)

    pixel_here_ids = jnp.arange(pixels_here) * devices + dev_index
    frame_keep = (
        jnp.arange(frame_total)[None, :] * P_SIZE + pixel_here_ids[:, None] < live_tokens[0]
    )
    frame_keep = frame_keep.reshape(pixels_here, 1, 1, frame_total)
    pixel_queries = by_pixel(parts[0])
    pixel_grad = by_pixel(parts[3])
    outcome = attend_forward(
        pixel_queries, by_pixel(parts[1]), by_pixel(parts[2]), pixel_grad, frame_keep
    )
    pixel_kgrad, pixel_vgrad = key_terms(pixel_queries, pixel_grad, outcome[2], outcome[3])
    temporal_grads = jnp.stack(
        [
            join_heads(
                lax.all_to_all(
                    back_rows(outcome[1]).astype(jnp.bfloat16),
                    "seq",
                    split_axis=0,
                    concat_axis=1,
                    tiled=True,
                )
            ),
            join_heads(
                lax.all_to_all(
                    back_rows(pixel_kgrad).astype(jnp.bfloat16),
                    "seq",
                    split_axis=0,
                    concat_axis=1,
                    tiled=True,
                )
            ),
            join_heads(
                lax.all_to_all(
                    back_rows(pixel_vgrad).astype(jnp.bfloat16),
                    "seq",
                    split_axis=0,
                    concat_axis=1,
                    tiled=True,
                )
            ),
        ]
    )
    caption_all = lax.all_gather(caption_kv, "seq", axis=0, tiled=True)
    caption_rows = caption_all.shape[0]
    caption_keys = caption_all[:, 0].reshape(1, caption_rows, head_count, HDIM)
    caption_values = caption_all[:, 1].reshape(1, caption_rows, head_count, HDIM)
    caption_keep = jnp.arange(caption_rows) < caption_len[0]
    cross_rows = split_heads(cross_query, 1)
    cross_grad = split_heads(grad_rows, 1)
    cross_results = attend_forward(
        cross_rows, caption_keys, caption_values, cross_grad, caption_keep
    )
    row_count = caption_kv.shape[0] * lax.axis_size("seq")
    slope_part = cross_results[3]
    weight_part = cross_results[2]
    key_part, value_part = key_terms(cross_rows, cross_grad, weight_part, slope_part)
    caption_grads = lax.psum_scatter(
        jnp.stack(
            [
                key_part.reshape(row_count, feature_width),
                value_part.reshape(row_count, feature_width),
            ],
            axis=1,
        ),
        "seq",
        scatter_dimension=0,
        tiled=True,
    )
    total_rows = (
        join_heads(spatial_out).astype(jnp.float32)
        + join_heads(
            lax.all_to_all(back_rows(outcome[0]), "seq", split_axis=0, concat_axis=1, tiled=True)
        ).astype(jnp.float32)
        + join_heads(cross_results[0]).astype(jnp.float32)
    )
    mixed = jnp.where(live_rows[:, None], total_rows, 0.0).astype(jnp.bfloat16)
    cross_query_grad = join_heads(cross_results[1]).astype(jnp.bfloat16)
    return (mixed, spatial_grads, temporal_grads, cross_query_grad, caption_grads)


def solution(mesh):
    placed = (
        P(None, ("dp", "seq"), None),
        P(None, ("dp", "seq"), None),
        P(("dp", "seq"), None),
        P(("dp", "seq"), None, None),
        P(("dp", "seq"), None),
        P("dp"),
        P("dp"),
    )
    return jax.shard_map(
        local,
        mesh=mesh,
        in_specs=placed,
        out_specs=(
            P(("dp", "seq"), None),
            P(None, ("dp", "seq"), None),
            P(None, ("dp", "seq"), None),
            P(("dp", "seq"), None),
            P(("dp", "seq"), None, None),
        ),
        check_vma=False,
    )
```

profile of v0, /device:TPU:2, one launch (start us, length us, event | category | flops | bytes accessed | tf_op | source)
XLA Modules:
  0.0 530.7 jit_solution(9359064735712591663)
XLA Ops:
  10.4 12.1 %all-to-all-start.4 = ((bf16[2,64,12,128]{3,0,2,1:T(2,128)(2,1)}), bf16[2,64,12,128]{3,0,2,1:T(2,128)(2,1)S(1)}, u32[]{:S(2)}, u32[]{:S(2)}) async-start(bf16[2,64,12,128]{3,0,2,1:T(2,128)(2,1)} %copy.125), calls=%async_computation.4 | async-start | bytes 786432 | tf_op jit(solution)/shard_map/all_to_all | solution.py:133
  25.2 11.8 %all-to-all-done.4 = bf16[2,64,12,128]{3,0,2,1:T(2,128)(2,1)S(1)} async-done(((bf16[2,64,12,128]{3,0,2,1:T(2,128)(2,1)}), bf16[2,64,12,128]{3,0,2,1:T(2,128)(2,1)S(1)}, u32[]{:S(2)}, u32[]{:S(2)}) %all-to-all-start.4) | async-done | bytes 393248 | tf_op jit(solution)/shard_map/all_to_all | solution.py:133
  37.0 6.3 %all-to-all-start = ((bf16[2,64,12,128]{3,0,2,1:T(2,128)(2,1)}), bf16[2,64,12,128]{3,0,2,1:T(2,128)(2,1)S(1)}, u32[]{:S(2)}, u32[]{:S(2)}) async-start(bf16[2,64,12,128]{3,0,2,1:T(2,128)(2,1)} %copy.94), calls=%async_computation | async-start | bytes 786432 | tf_op jit(solution)/shard_map/all_to_all | solution.py:124
  44.7 13.1 %all-to-all-done = bf16[2,64,12,128]{3,0,2,1:T(2,128)(2,1)S(1)} async-done(((bf16[2,64,12,128]{3,0,2,1:T(2,128)(2,1)}), bf16[2,64,12,128]{3,0,2,1:T(2,128)(2,1)S(1)}, u32[]{:S(2)}, u32[]{:S(2)}) %all-to-all-start) | async-done | bytes 393248 | tf_op jit(solution)/shard_map/all_to_all | solution.py:124
  57.9 6.3 %all-to-all-start.2 = ((bf16[2,64,12,128]{3,0,2,1:T(2,128)(2,1)}), bf16[2,64,12,128]{3,0,2,1:T(2,128)(2,1)S(1)}, u32[]{:S(2)}, u32[]{:S(2)}) async-start(bf16[2,64,12,128]{3,0,2,1:T(2,128)(2,1)} %copy.100), calls=%async_computation.2 | async-start | bytes 786432 | tf_op jit(solution)/shard_map/all_to_all | solution.py:130
  65.6 13.1 %all-to-all-done.2 = bf16[2,64,12,128]{3,0,2,1:T(2,128)(2,1)S(1)} async-done(((bf16[2,64,12,128]{3,0,2,1:T(2,128)(2,1)}), bf16[2,64,12,128]{3,0,2,1:T(2,128)(2,1)S(1)}, u32[]{:S(2)}, u32[]{:S(2)}) %all-to-all-start.2) | async-done | bytes 393248 | tf_op jit(solution)/shard_map/all_to_all | solution.py:130
  78.7 6.5 %all-to-all-start.1 = ((bf16[2,64,12,128]{3,0,2,1:T(2,128)(2,1)}), bf16[2,64,12,128]{3,0,2,1:T(2,128)(2,1)}, u32[]{:S(2)}, u32[]{:S(2)}) async-start(bf16[2,64,12,128]{3,0,2,1:T(2,128)(2,1)} %copy.97), calls=%async_computation.1 | async-start | bytes 786432 | tf_op jit(solution)/shard_map/all_to_all | solution.py:127
  87.6 12.0 %all-to-all-done.1 = bf16[2,64,12,128]{3,0,2,1:T(2,128)(2,1)} async-done(((bf16[2,64,12,128]{3,0,2,1:T(2,128)(2,1)}), bf16[2,64,12,128]{3,0,2,1:T(2,128)(2,1)}, u32[]{:S(2)}, u32[]{:S(2)}) %all-to-all-start.1) | async-done | bytes 393248 | tf_op jit(solution)/shard_map/all_to_all | solution.py:127
  105.2 6.4 %all-to-all-start.7 = ((bf16[128,1,12,128]{3,2,1,0:T(8,128)(2,1)}), bf16[128,1,12,128]{3,2,1,0:T(8,128)(2,1)S(1)}, u32[]{:S(2)}, u32[]{:S(2)}) async-start(bf16[128,1,12,128]{3,2,1,0:T(8,128)(2,1)} %copy.139), calls=%async_computation.7 | async-start | bytes 1048576 | tf_op jit(solution)/shard_map/all_to_all | solution.py:177
  116.3 12.6 %all-to-all-done.7 = bf16[128,1,12,128]{3,2,1,0:T(8,128)(2,1)S(1)} async-done(((bf16[128,1,12,128]{3,2,1,0:T(8,128)(2,1)}), bf16[128,1,12,128]{3,2,1,0:T(8,128)(2,1)S(1)}, u32[]{:S(2)}, u32[]{:S(2)}) %all-to-all-start.7) | async-done | bytes 393248 | tf_op jit(solution)/shard_map/all_to_all | solution.py:177
  128.9 6.4 %all-to-all-start.6 = ((bf16[128,1,12,128]{3,2,1,0:T(8,128)(2,1)}), bf16[128,1,12,128]{3,2,1,0:T(8,128)(2,1)S(1)}, u32[]{:S(2)}, u32[]{:S(2)}) async-start(bf16[128,1,12,128]{3,2,1,0:T(8,128)(2,1)} %copy.135), calls=%async_computation.6 | async-start | bytes 1048576 | tf_op jit(solution)/shard_map/all_to_all | solution.py:168
  137.9 14.5 %all-to-all-done.6 = bf16[128,1,12,128]{3,2,1,0:T(8,128)(2,1)S(1)} async-done(((bf16[128,1,12,128]{3,2,1,0:T(8,128)(2,1)}), bf16[128,1,12,128]{3,2,1,0:T(8,128)(2,1)S(1)}, u32[]{:S(2)}, u32[]{:S(2)}) %all-to-all-start.6) | async-done | bytes 393248 | tf_op jit(solution)/shard_map/all_to_all | solution.py:168
  152.4 6.8 %all-to-all-start.5 = ((bf16[128,1,12,128]{3,2,1,0:T(8,128)(2,1)}), bf16[128,1,12,128]{3,2,1,0:T(8,128)(2,1)}, u32[]{:S(2)}, u32[]{:S(2)}) async-start(bf16[128,1,12,128]{3,2,1,0:T(8,128)(2,1)} %copy.131), calls=%async_computation.5 | async-start | bytes 1048576 | tf_op jit(solution)/shard_map/all_to_all | solution.py:159
  164.0 12.3 %all-to-all-done.5 = bf16[128,1,12,128]{3,2,1,0:T(8,128)(2,1)} async-done(((bf16[128,1,12,128]{3,2,1,0:T(8,128)(2,1)}), bf16[128,1,12,128]{3,2,1,0:T(8,128)(2,1)}, u32[]{:S(2)}, u32[]{:S(2)}) %all-to-all-start.5) | async-done | bytes 393248 | tf_op jit(solution)/shard_map/all_to_all | solution.py:159
  176.3 6.9 %all-to-all-start.3 = ((bf16[128,1,12,128]{3,2,1,0:T(8,128)(2,1)}), bf16[128,1,12,128]{3,2,1,0:T(8,128)(2,1)}, u32[]{:S(2)}, u32[]{:S(2)}) async-start(bf16[128,1,12,128]{3,2,1,0:T(8,128)(2,1)} %copy.105), calls=%async_computation.3 | async-start | bytes 1048576 | tf_op jit(solution)/shard_map/all_to_all | solution.py:216
  191.7 30.3 %all-to-all-done.3 = bf16[128,1,12,128]{3,2,1,0:T(8,128)(2,1)} async-done(((bf16[128,1,12,128]{3,2,1,0:T(8,128)(2,1)}), bf16[128,1,12,128]{3,2,1,0:T(8,128)(2,1)}, u32[]{:S(2)}, u32[]{:S(2)}) %all-to-all-start.3) | async-done | bytes 393248 | tf_op jit(solution)/shard_map/all_to_all | solution.py:216
  239.7 25.5 %all-gather.2.cloned.1.call-done = bf16[320,2,1536]{2,1,0:T(2,128)(2,1)} async-done(((bf16[5,2,1536]{2,1,0:T(2,128)(2,1)}), bf16[320,2,1536]{2,1,0:T(2,128)(2,1)}) %all-gather.2.cloned.1.call-update) | async-done | bytes 1966096 | tf_op jit(solution)/shard_map/all_gather | solution.py:187
  265.2 6.7 %fusion.71 = (bf16[320,1,1536]{2,1,0:T(2,128)(2,1)}, bf16[320,1,1536]{2,1,0:T(2,128)(2,1)}) fusion(bf16[320,2,1536]{2,1,0:T(2,128)(2,1)} %all-gather.2.cloned.1.call-done), kind=kLoop, calls=%fused_computation.109 | loop fusion | bytes 3932160 | tf_op jit(solution)/shard_map/slice | solution.py:189
  271.9 4.9 copy.110
  276.8 5.0 copy.113
  313.4 4.8 pad_maximum_fusion
  318.2 8.1 %copy.151 = f32[320,2,1536]{2,1,0:T(2,128)} copy(f32[320,2,1536]{0,2,1:T(8,128)} %pad_maximum_fusion) | data formatting | bytes 7864320 | tf_op jit(solution)/shard_map/stack | solution.py:202
  330.9 8.4 %collective-permute-done.2 = bf16[2,256,1536]{1,2,0:T(8,128)(2,1)} collective-permute-done((bf16[2,256,1536]{1,2,0:T(8,128)(2,1)}, bf16[2,256,1536]{1,2,0:T(8,128)(2,1)}, u32[]{:S(2)}, u32[]{:S(2)}) %collective-permute-start.2) | collective-permute-done | bytes 1572896 | tf_op jit(solution)/shard_map/ppermute | solution.py:11
  351.6 167.5 %all-reduce.3.cloned.1.call-done = f32[320,2,1536]{2,1,0:T(2,128)} async-done(((f32[320,2,1536]{2,1,0:T(2,128)}), f32[320,2,1536]{2,1,0:T(2,128)}) %all-reduce.3.cloned.1.call-update) | async-done | bytes 3932176
  (178 shorter events, 105.5 us)
Async XLA Ops:
  10.4 26.7 %all-to-all-start.4 = ((bf16[2,64,12,128]{3,0,2,1:T(2,128)(2,1)}), bf16[2,64,12,128]{3,0,2,1:T(2,128)(2,1)S(1)}, u32[]{:S(2)}, u32[]{:S(2)}) async-start(bf16[2,64,12,128]{3,0,2,1:T(2,128)(2,1)} %copy.125), calls=%async_computation.4 | async-start | bytes 786432 | tf_op jit(solution)/shard_map/all_to_all | solution.py:133
  37.0 27.1 %copy-start.21 = (bf16[2,64,12,128]{3,0,2,1:T(2,128)(2,1)}, bf16[2,64,12,128]{3,0,2,1:T(2,128)(2,1)S(1)}, u32[]{:S(2)}) copy-start(bf16[2,64,12,128]{3,0,2,1:T(2,128)(2,1)S(1)} %all-to-all-done.4) | copy-start | bytes 1179652
  37.0 20.8 %all-to-all-start = ((bf16[2,64,12,128]{3,0,2,1:T(2,128)(2,1)}), bf16[2,64,12,128]{3,0,2,1:T(2,128)(2,1)S(1)}, u32[]{:S(2)}, u32[]{:S(2)}) async-start(bf16[2,64,12,128]{3,0,2,1:T(2,128)(2,1)} %copy.94), calls=%async_computation | async-start | bytes 786432 | tf_op jit(solution)/shard_map/all_to_all | solution.py:124
  57.9 20.8 %all-to-all-start.2 = ((bf16[2,64,12,128]{3,0,2,1:T(2,128)(2,1)}), bf16[2,64,12,128]{3,0,2,1:T(2,128)(2,1)S(1)}, u32[]{:S(2)}, u32[]{:S(2)}) async-start(bf16[2,64,12,128]{3,0,2,1:T(2,128)(2,1)} %copy.100), calls=%async_computation.2 | async-start | bytes 786432 | tf_op jit(solution)/shard_map/all_to_all | solution.py:130
  64.2 21.0 %slice-start = ((bf16[3,128,1536]{2,1,0:T(8,128)(2,1)}), bf16[2,128,1536]{2,1,0:T(8,128)(2,1)S(1)}, s32[]{:S(2)}) async-start(bf16[3,128,1536]{2,1,0:T(8,128)(2,1)} %param.7), calls=%async_computation.10 | async-start | bytes 1572864 | tf_op jit(solution)/shard_map/slice | solution.py:91
  65.6 20.2 %copy-start.22 = (bf16[2,64,12,128]{3,0,2,1:T(2,128)(2,1)S(1)}, bf16[2,64,12,128]{3,0,2,1:T(2,128)(2,1)}, u32[]{:S(2)}) copy-start(bf16[2,64,12,128]{3,0,2,1:T(2,128)(2,1)} %copy-done.21) | copy-start | bytes 1179652
  78.7 20.9 %all-to-all-start.1 = ((bf16[2,64,12,128]{3,0,2,1:T(2,128)(2,1)}), bf16[2,64,12,128]{3,0,2,1:T(2,128)(2,1)}, u32[]{:S(2)}, u32[]{:S(2)}) async-start(bf16[2,64,12,128]{3,0,2,1:T(2,128)(2,1)} %copy.97), calls=%async_computation.1 | async-start | bytes 786432 | tf_op jit(solution)/shard_map/all_to_all | solution.py:127
  85.6 73.7 %collective-permute-start = (bf16[2,128,1536]{1,2,0:T(8,128)(2,1)S(1)}, bf16[2,128,1536]{1,2,0:T(8,128)(2,1)}, u32[]{:S(2)}, u32[]{:S(2)}) collective-permute-start(bf16[2,128,1536]{1,2,0:T(8,128)(2,1)S(1)} %copy.202), channel_id=1, source_target_pairs={{0,1},{1,0},{2,3},{3,2},{4,5},{5,4},{6,7},{7,6},{8,9},{9,8},{10,11... | collective-permute-start | bytes 2359304 | tf_op jit(solution)/shard_map/ppermute | solution.py:11
  86.1 16.3 %copy-start.30 = (bf16[64,2,1,12,128]{4,1,0,3,2:T(2,128)(2,1)}, bf16[64,2,1,12,128]{4,1,0,3,2:T(2,128)(2,1)S(1)}, u32[]{:S(2)}) copy-start(bf16[64,2,1,12,128]{4,1,0,3,2:T(2,128)(2,1)S(1)} %copy.126) | copy-start | bytes 1179652
  105.2 23.6 %all-to-all-start.7 = ((bf16[128,1,12,128]{3,2,1,0:T(8,128)(2,1)}), bf16[128,1,12,128]{3,2,1,0:T(8,128)(2,1)S(1)}, u32[]{:S(2)}, u32[]{:S(2)}) async-start(bf16[128,1,12,128]{3,2,1,0:T(8,128)(2,1)} %copy.139), calls=%async_computation.7 | async-start | bytes 1048576 | tf_op jit(solution)/shard_map/all_to_all | solution.py:177
  128.9 23.6 %all-to-all-start.6 = ((bf16[128,1,12,128]{3,2,1,0:T(8,128)(2,1)}), bf16[128,1,12,128]{3,2,1,0:T(8,128)(2,1)S(1)}, u32[]{:S(2)}, u32[]{:S(2)}) async-start(bf16[128,1,12,128]{3,2,1,0:T(8,128)(2,1)} %copy.135), calls=%async_computation.6 | async-start | bytes 1048576 | tf_op jit(solution)/shard_map/all_to_all | solution.py:168
  152.4 23.8 %all-to-all-start.5 = ((bf16[128,1,12,128]{3,2,1,0:T(8,128)(2,1)}), bf16[128,1,12,128]{3,2,1,0:T(8,128)(2,1)}, u32[]{:S(2)}, u32[]{:S(2)}) async-start(bf16[128,1,12,128]{3,2,1,0:T(8,128)(2,1)} %copy.131), calls=%async_computation.5 | async-start | bytes 1048576 | tf_op jit(solution)/shard_map/all_to_all | solution.py:159
  161.1 64.6 %collective-permute-start.1 = (bf16[2,256,1536]{1,2,0:T(8,128)(2,1)S(1)}, bf16[2,256,1536]{1,2,0:T(8,128)(2,1)}, u32[]{:S(2)}, u32[]{:S(2)}) collective-permute-start(bf16[2,256,1536]{1,2,0:T(8,128)(2,1)S(1)} %maximum_select_fusion.1), channel_id=1, source_target_pairs={{0,2},{1,3},{2,0},{3,1},{4,6},{5,7},{6,4},{7,5},{8,10},{9,11},{10,... | collective-permute-start | bytes 4718600 | tf_op jit(solution)/shard_map/ppermute | solution.py:11
  162.9 22.7 %copy-start.28 = (bf16[128,1536]{1,0:T(8,128)(2,1)S(1)}, bf16[128,1536]{1,0:T(8,128)(2,1)}, u32[]{:S(2)}) copy-start(bf16[128,1536]{1,0:T(8,128)(2,1)} %param.9) | copy-start | bytes 1179652
  164.0 22.6 %slice-start.1 = ((bf16[3,128,1536]{2,1,0:T(8,128)(2,1)}), bf16[1,128,1536]{2,1,0:T(8,128)(2,1)S(1)}, s32[]{:S(2)}) async-start(bf16[3,128,1536]{2,1,0:T(8,128)(2,1)} %param.7), calls=%async_computation.11 | async-start | bytes 786432 | tf_op jit(solution)/shard_map/slice | solution.py:96
  164.0 23.5 %copy-start.34 = (u32[256]{0:T(256)S(1)}, u32[256]{0:T(256)}, u32[]{:S(2)}) copy-start(u32[256]{0:T(256)} %constant.88) | copy-start | bytes 3076
  164.0 24.7 %copy-start.12 = (bf16[128,1,12,128]{3,2,1,0:T(8,128)(2,1)S(1)}, bf16[128,1,12,128]{3,2,1,0:T(8,128)(2,1)}, u32[]{:S(2)}) copy-start(bf16[128,1,12,128]{3,2,1,0:T(8,128)(2,1)} %copy-done.11) | copy-start | bytes 1179652
  176.3 45.7 %all-to-all-start.3 = ((bf16[128,1,12,128]{3,2,1,0:T(8,128)(2,1)}), bf16[128,1,12,128]{3,2,1,0:T(8,128)(2,1)}, u32[]{:S(2)}, u32[]{:S(2)}) async-start(bf16[128,1,12,128]{3,2,1,0:T(8,128)(2,1)} %copy.105), calls=%async_computation.3 | async-start | bytes 1048576 | tf_op jit(solution)/shard_map/all_to_all | solution.py:216
  183.2 82.0 %all-gather.2.cloned.1.call-start = ((), (), s32[]{:S(2)}) async-start(), calls=%async_computation.8 | async-start | bytes 1996800 | tf_op jit(solution)/shard_map/all_gather | solution.py:187
  183.9 335.2 %all-reduce.3.cloned.1.call-start = ((), (), s32[]{:S(2)}) async-start(), calls=%async_computation.9 | async-start | bytes 7864320
  301.8 37.5 %collective-permute-start.2 = (bf16[2,256,1536]{1,2,0:T(8,128)(2,1)}, bf16[2,256,1536]{1,2,0:T(8,128)(2,1)}, u32[]{:S(2)}, u32[]{:S(2)}) collective-permute-start(bf16[2,256,1536]{1,2,0:T(8,128)(2,1)} %fusion.4), channel_id=1, source_target_pairs={{0,2},{1,3},{2,0},{3,1},{4,6},{5,7},{6,4},{7,5},{8,10},{9,11},{10,... | collective-permute-start | bytes 4718600 | tf_op jit(solution)/shard_map/ppermute | solution.py:11
  328.3 11.0 %copy-start = (f32[1,512,12,128]{1,3,2,0:T(8,128)S(1)}, f32[1,512,12,128]{1,3,2,0:T(8,128)}, u32[]{:S(2)}) copy-start(f32[1,512,12,128]{1,3,2,0:T(8,128)} %copy.123) | copy-start | bytes 9437188
  343.9 176.6 %collective-permute-start.3 = (bf16[2,128,1536]{1,2,0:T(8,128)(2,1)}, bf16[2,128,1536]{1,2,0:T(8,128)(2,1)}, u32[]{:S(2)}, u32[]{:S(2)}) collective-permute-start(bf16[2,128,1536]{1,2,0:T(8,128)(2,1)} %dynamic-slice_convert_fusion), channel_id=1, source_target_pairs={{0,1},{1,0},{2,3},{3,2},{4,5},{5,4},{6,7},{7,6},{8,9},{9,8},{10,11... | collective-permute-start | bytes 2359304 | tf_op jit(solution)/shard_map/ppermute | solution.py:11
  346.3 174.2 %copy-start.3 = (f32[2,256,1536]{1,2,0:T(8,128)S(1)}, f32[2,256,1536]{1,2,0:T(8,128)}, u32[]{:S(2)}) copy-start(f32[2,256,1536]{1,2,0:T(8,128)} %copy-done.2) | copy-start | bytes 9437188
  (32 other events, 109.1 us)
Sparse Core Ops, SparseCore 0:
  186.7 78.4 all-gather.1
  326.4 192.6 all-reduce.2
where the time goes:
time: 541 us; the launch traced here: 531 us
  waiting for transfers between devices  322 us (60%)
  local copies, waits for them, and re-layouts  74.8 us (14%)
  starting transfers between devices  60.1 us (11%)
  matrix products  32.8 us (6%)
  other arithmetic  24.3 us (4%)
  between operations  17.1 us (3%)
    unnamed x3, waiting for transfers between devices  168 us
    all_to_all x1, waiting for transfers between devices, local(): lax.all_to_all(back_rows(outcome[0]), 'seq', split_axis=0, concat_axis=1,...  30.3 us
    all_gather x1, waiting for transfers between devices, local(): caption_all = lax.all_gather(caption_kv, 'seq', axis=0, tiled=True)  25.5 us
    unnamed x88, local copies, waits for them, and re-layouts  14.5 us
    all_to_all x1, waiting for transfers between devices, local(): lax.all_to_all(back_rows(pixel_kgrad).astype(jnp.bfloat16), 'seq', split_...  14.5 us
    all_to_all x1, waiting for transfers between devices, local(): lax.all_to_all(pixel_split(temporal_qkv[0]), 'seq', split_axis=1, concat_...  13.1 us
    all_to_all x1, waiting for transfers between devices, local(): lax.all_to_all(pixel_split(temporal_qkv[2]), 'seq', split_axis=1, concat_...  13.1 us
    all_to_all x1, waiting for transfers between devices, local(): lax.all_to_all(back_rows(pixel_vgrad).astype(jnp.bfloat16), 'seq', split_...  12.6 us
  transfers between devices with their start and end apart: 14, of which 11 were waited for; matrix products, arithmetic and copies ran while one was open for 16% of the time, Pallas kernels for 0%

commit v1 on v0

v1 whole, which is shorter than its diff:
```python
import functools

import jax
import jax.numpy as jnp
from jax import lax
from jax.experimental import pallas as pl
from jax.experimental.pallas import tpu as pltpu
from jax.sharding import PartitionSpec as P

HDIM = 128
ROWS = 128
WIDTH = 1536
FRAME_ROWS = 512
QUARTER = 384
HALF = 768
PIXELS = 16
FRAMES = 16
CAP_ROWS = 320
CAP_PAD = 32
MESSAGE = 5 * ROWS + 2 * CAP_PAD
SCALE = HDIM**-0.5
EXP2_SCALE = SCALE * 1.4426950408889634
BF16 = jnp.bfloat16
F32 = jnp.float32
VMEM_LIMIT = 48 * 2**20


def dot_nt(a, b):
    return lax.dot_general(a, b, (((1,), (1,)), ((), ())), preferred_element_type=F32)


def dot_tn(a, b):
    return lax.dot_general(a, b, (((0,), (0,)), ((), ())), preferred_element_type=F32)


def dot_nn(a, b):
    return lax.dot_general(a, b, (((1,), (0,)), ((), ())), preferred_element_type=F32)


def attend(q, k, v, g, keep=None):
    scores = dot_nt(k, q)
    if keep is not None:
        scores = jnp.where(keep, scores, -1e30)
    largest = jnp.max(scores, axis=0, keepdims=True)
    raised = jnp.exp2((scores - largest) * EXP2_SCALE)
    weights = raised * (1.0 / jnp.sum(raised, axis=0, keepdims=True))
    weights_low = weights.astype(BF16)
    dprobs = dot_nt(v, g)
    row_delta = jnp.sum(weights * dprobs, axis=0, keepdims=True)
    slopes = (weights * (dprobs - row_delta)).astype(BF16)
    out = dot_tn(weights_low, v)
    dq = dot_tn(slopes, k) * SCALE
    dk = dot_nn(slopes, q) * SCALE
    dv = dot_nn(weights_low, g)
    return out, dq, dk, dv


def frame_pack_kernel(scal, sqkv, grad, cq, *outs):
    for step, out in enumerate(outs):
        block = jnp.bitwise_xor(scal[0], step)
        lanes = pl.ds(pl.multiple_of(block * QUARTER, 128), QUARTER)
        for i in range(3):
            out[i * ROWS : (i + 1) * ROWS, :] = sqkv[i, :, lanes]
        out[3 * ROWS : 4 * ROWS, :] = grad[:, lanes]
        out[4 * ROWS : 5 * ROWS, :] = cq[:, lanes]


def temporal_pack_kernel(tqkv, grad, out):
    for group in range(8):
        rows = slice(group * PIXELS, (group + 1) * PIXELS)
        for half in range(2):
            lanes = slice(half * HALF, (half + 1) * HALF)
            for i in range(3):
                out[2 * group + half, i * PIXELS : (i + 1) * PIXELS, :] = tqkv[i, rows, lanes]
            out[2 * group + half, 3 * PIXELS : 4 * PIXELS, :] = grad[rows, lanes]


def live_grads(scal, parts):
    row = lax.broadcasted_iota(jnp.int32, (ROWS, HDIM), 0)
    grads = []
    for step, part in enumerate(parts):
        first = (scal[1] * 4 + jnp.bitwise_xor(scal[0], step)) * ROWS
        grads.append(jnp.where(row + first < scal[2], part.astype(F32), 0.0).astype(BF16))
    return jnp.concatenate(grads, axis=0)


def put_rows(outs, i, item):
    item = item.astype(BF16)
    for step, out in enumerate(outs):
        out[i * ROWS : (i + 1) * ROWS, :] = item[step * ROWS : (step + 1) * ROWS, :]


def spatial_kernel(scal, m0, m1, m2, m3, *outs):
    parts = (m0, m1, m2, m3)

    def joined(i):
        return jnp.concatenate([part[i * ROWS : (i + 1) * ROWS, :] for part in parts], axis=0)

    g = live_grads(scal, [part[3 * ROWS : 4 * ROWS, :] for part in parts])
    out, *grads = attend(joined(0), joined(1), joined(2), g)
    put_rows(outs, 0, out)
    for i, item in enumerate(grads):
        put_rows(outs, i + 2, item)


def cap_pack_kernel(scal, caps, m0, m1, m2, m3, *outs):
    for step, out in enumerate(outs):
        block = jnp.bitwise_xor(scal[0], step)
        lanes = pl.ds(pl.multiple_of(block * QUARTER, 128), QUARTER)
        for kind in range(2):
            out[kind * CAP_PAD : (kind + 1) * CAP_PAD, :] = caps[kind, :, lanes]


def cap_join_kernel(m0, m1, m2, m3, out, rows):
    for i, part in enumerate((m0, m1, m2, m3)):
        for kind in range(2):
            item = part[kind * CAP_PAD : (kind + 1) * CAP_PAD, :].astype(F32)
            rows[20 * i : 20 * (i + 1), kind * QUARTER : (kind + 1) * QUARTER] = item[:20]
    out[...] = rows[...].astype(BF16)


def cap_sum_y_kernel(p0, p1, p2, p3, o0, o1, o2, o3, rows, picked):
    rows[...] = sum(part[...].astype(F32) for part in (p0, p1, p2, p3))
    for z, out in enumerate((o0, o1, o2, o3)):
        for s in range(4):
            first = 20 * s + 5 * z
            picked[:, 5 * s : 5 * (s + 1), :] = rows[:, first : first + 5, :]
        out[...] = picked[...].astype(BF16)


def cap_sum_z_kernel(p0, p1, p2, p3, o0, o1, o2, o3, rows):
    rows[...] = sum(part[...].astype(F32) for part in (p0, p1, p2, p3))
    for s, out in enumerate((o0, o1, o2, o3)):
        out[...] = rows[:, 5 * s : 5 * s + 8, :]


def cap_place_kernel(scal, p0, p1, p2, p3, out):
    for step, part in enumerate((p0, p1, p2, p3)):
        block = jnp.bitwise_xor(scal[0], step)
        lanes = pl.ds(pl.multiple_of(block * QUARTER, 128), QUARTER)
        for kind in range(2):
            out[kind, :, lanes] = part[kind]


def cross_kernel(
    scal, g0, g1, g2, g3, q0, q1, q2, q3, c0, c1, c2, c3, d0, d1, d2, d3, s0, s1, s2, s3, *outs
):
    spatial = jnp.concatenate([s[0:ROWS, :] for s in (s0, s1, s2, s3)], axis=0)
    queries = jnp.concatenate([q0[...], q1[...], q2[...], q3[...]], axis=0)
    keys = jnp.concatenate([c0[...], c1[...], c2[...], c3[...]], axis=0)
    values = jnp.concatenate([d0[...], d1[...], d2[...], d3[...]], axis=0)
    g = live_grads(scal, [g0[...], g1[...], g2[...], g3[...]])
    slot = lax.broadcasted_iota(jnp.int32, (CAP_ROWS, 1), 0)
    five = jnp.right_shift(slot * 205, 10)
    owner_y = jnp.bitwise_and(jnp.right_shift(five, 4) + jnp.right_shift(scal[1], 2), 3)
    owner_z = jnp.bitwise_and(five + scal[1], 3)
    peer = jnp.bitwise_and(jnp.right_shift(five, 2), 3)
    owner = (owner_y * 4 + owner_z) * 4 + jnp.bitwise_xor(peer, scal[0])
    keep = owner * 5 + (slot - five * 5) < scal[3]
    out, dq, dk, dv = attend(queries, keys, values, g, keep)
    put_rows(outs[:4], 0, out + spatial.astype(F32))
    put_rows(outs[:4], 1, dq)
    for i in range(4):
        outs[4 + i][0, :, :] = dk[80 * i : 80 * (i + 1)].astype(BF16)
        outs[4 + i][1, :, :] = dv[80 * i : 80 * (i + 1)].astype(BF16)


def temporal_kernel(scal, block, out):
    size = FRAMES * PIXELS

    def rows_of(i):
        return block[:, i * PIXELS : (i + 1) * PIXELS, :].reshape(size, HDIM)

    first = scal[0] * ROWS + (scal[1] // 2) * PIXELS

    def token(shape, dim):
        place = lax.broadcasted_iota(jnp.int32, shape, dim)
        pixel = jnp.bitwise_and(place, PIXELS - 1)
        return pixel, (place // PIXELS) * FRAME_ROWS + first + pixel

    key_pixel, key_token = token((size, size), 0)
    query_pixel, _ = token((size, size), 1)
    keep = jnp.logical_and(key_pixel == query_pixel, key_token < scal[2])
    _, row_token = token((size, HDIM), 0)
    g = jnp.where(row_token < scal[2], rows_of(3).astype(F32), 0.0).astype(BF16)
    for i, item in enumerate(attend(rows_of(0), rows_of(1), rows_of(2), g, keep)):
        out[:, i * PIXELS : (i + 1) * PIXELS, :] = item.astype(BF16).reshape(FRAMES, PIXELS, HDIM)


def frame_unpack_kernel(scal, m0, m1, m2, m3, both, grads, cross_grad):
    for step, part in enumerate((m0, m1, m2, m3)):
        block = jnp.bitwise_xor(scal[0], step)
        lanes = pl.ds(pl.multiple_of(block * QUARTER, 128), QUARTER)
        both[:, lanes] = part[0:ROWS, :]
        cross_grad[:, lanes] = part[ROWS : 2 * ROWS, :]
        for i in range(3):
            grads[i, :, lanes] = part[(i + 2) * ROWS : (i + 3) * ROWS, :]


def temporal_unpack_kernel(scal, back, both, mixed, grads):
    first = (scal[1] * 4 + scal[0]) * ROWS + pl.program_id(0) * PIXELS * (back.shape[0] // 2)
    row = lax.broadcasted_iota(jnp.int32, (PIXELS, HALF), 0)
    for group in range(back.shape[0] // 2):
        rows = slice(group * PIXELS, (group + 1) * PIXELS)
        live = row + (first + group * PIXELS) < scal[2]
        for half in range(2):
            lanes = slice(half * HALF, (half + 1) * HALF)
            t = 2 * group + half
            total = back[t, 0:PIXELS, :].astype(F32) + both[rows, lanes].astype(F32)
            mixed[rows, lanes] = jnp.where(live, total, 0.0).astype(BF16)
            for i in range(3):
                grads[i, rows, lanes] = back[t, (i + 1) * PIXELS : (i + 2) * PIXELS, :]


def spec(shape=None, index=None):
    if shape is None:
        return pl.BlockSpec(memory_space=pltpu.VMEM)
    return pl.BlockSpec(shape, index)


SMEM = pl.BlockSpec(memory_space=pltpu.SMEM)


def call(
    kernel,
    out_shape,
    in_specs,
    out_specs,
    grid=None,
    flops=0,
    moved=0,
    name=None,
    after=(),
    scratch=(),
    aliases=None,
):
    options = {} if grid is None else {"grid": grid}
    known = len(in_specs)

    def body(*refs):
        kernel(*refs[:known], *refs[known + len(after) :])

    made = pl.pallas_call(
        body,
        out_shape=out_shape,
        in_specs=list(in_specs) + [pl.BlockSpec(memory_space=pl.ANY)] * len(after),
        out_specs=out_specs,
        scratch_shapes=list(scratch),
        input_output_aliases=aliases or {},
        compiler_params=pltpu.CompilerParams(vmem_limit_bytes=VMEM_LIMIT),
        cost_estimate=pl.CostEstimate(flops=flops, bytes_accessed=moved, transcendentals=0),
        name=name,
        **options,
    )
    return lambda *args: made(*args, *after)


def gate(arrays, after):
    anywhere = pl.BlockSpec(memory_space=pl.ANY)
    count = len(arrays)
    return pl.pallas_call(
        lambda *refs: None,
        out_shape=[jax.ShapeDtypeStruct(a.shape, a.dtype) for a in arrays],
        in_specs=[anywhere] * (count + len(after)),
        out_specs=[anywhere] * count,
        input_output_aliases={i: i for i in range(count)},
        compiler_params=pltpu.CompilerParams(vmem_limit_bytes=VMEM_LIMIT),
        cost_estimate=pl.CostEstimate(flops=0, bytes_accessed=1000, transcendentals=0),
        name="gate",
    )(*arrays, *after)


def low(*shape):
    return jax.ShapeDtypeStruct(shape, BF16)


def full(*shape):
    return jax.ShapeDtypeStruct(shape, F32)


def place(y, z, r):
    return (y % 4) * 16 + (z % 4) * 4 + r


def shifted(dy, dz):
    return [
        (place(y, z, r), place(y + dy, z + dz, r))
        for y in range(4)
        for z in range(4)
        for r in range(4)
    ]


def crossed(step):
    return [(i, i ^ step) for i in range(64)]


GROUPS = [[4 * f + r for f in range(16)] for r in range(4)]


def local(spatial_qkv, temporal_qkv, cross_query, caption_kv, out_grad, live_tokens, caption_len):
    index = lax.axis_index("seq").astype(jnp.int32)
    me, frame = index % 4, index // 4
    scal = jnp.stack([me, frame, live_tokens[0], caption_len[0]])

    caps = [caption_kv] + [lax.ppermute(caption_kv, "seq", shifted(0, -s)) for s in (1, 2, 3)]

    packs = call(
        frame_pack_kernel,
        [low(MESSAGE, QUARTER)] * 4,
        [SMEM] + [spec()] * 3,
        [spec((5 * ROWS, QUARTER), lambda i: (0, 0))] * 4,
        grid=(1,),
        moved=1000,
        name="frame_pack",
    )(scal, spatial_qkv, out_grad, cross_query)
    sent = call(
        temporal_pack_kernel,
        low(16, 4 * PIXELS, HALF),
        [spec()] * 2,
        spec(),
        moved=1000,
        name="temporal_pack",
        after=(packs[0],),
    )(temporal_qkv, out_grad)
    caps = jnp.swapaxes(jnp.concatenate(caps, axis=0), 0, 1)
    caps = jnp.pad(caps, ((0, 0), (0, CAP_PAD - 20), (0, 0)))
    cap_rows = spec((2 * CAP_PAD, QUARTER), lambda i: (5 * ROWS // (2 * CAP_PAD), 0))
    packs = call(
        cap_pack_kernel,
        [low(MESSAGE, QUARTER)] * 4,
        [SMEM, spec()] + [pl.BlockSpec(memory_space=pl.ANY)] * 4,
        [cap_rows] * 4,
        grid=(1,),
        moved=1000,
        name="cap_pack",
        after=(sent,),
        aliases={2 + i: i for i in range(4)},
    )(scal, caps, *packs)
    got = [packs[0]] + [lax.ppermute(packs[s], "seq", crossed(s)) for s in (1, 2, 3)]

    (sent,) = gate([sent], [packs[0]])
    block = lax.all_to_all(
        sent, "seq", split_axis=0, concat_axis=0, tiled=True, axis_index_groups=GROUPS
    )

    message = spec((MESSAGE, HDIM), lambda h: (0, h))
    result = spec((5 * ROWS, HDIM), lambda h: (0, h))
    spatial = call(
        spatial_kernel,
        [low(5 * ROWS, QUARTER)] * 4,
        [SMEM] + [message] * 4,
        [result] * 4,
        grid=(3,),
        flops=100_000_000_000,
        moved=4_000_000,
        name="spatial_attention",
    )(scal, *got)

    caps = call(
        cap_join_kernel,
        low(80, HALF),
        [cap_rows] * 4,
        spec((80, HALF), lambda i: (0, 0)),
        grid=(1,),
        moved=300_000,
        name="cap_join",
        after=(spatial[0],),
        scratch=[pltpu.VMEM((80, HALF), F32)],
    )(*got)
    caps = [caps] + [lax.ppermute(caps, "seq", shifted(-s, 0)) for s in (1, 2, 3)]

    front = spec((2 * ROWS, HDIM), lambda h: (0, h))
    *done, c0, c1, c2, c3 = call(
        cross_kernel,
        [low(5 * ROWS, QUARTER)] * 4 + [low(2, 80, QUARTER)] * 4,
        [SMEM]
        + [spec((ROWS, HDIM), lambda h: (3, h))] * 4
        + [spec((ROWS, HDIM), lambda h: (4, h))] * 4
        + [spec((80, HDIM), lambda h: (0, h))] * 4
        + [spec((80, HDIM), lambda h: (0, h + 3))] * 4
        + [front] * 4,
        [front] * 4 + [spec((2, 80, HDIM), lambda h: (0, 0, h))] * 4,
        grid=(3,),
        flops=1_000_000_000,
        moved=3_000_000,
        name="cross_attention",
        aliases={17 + i: i for i in range(4)},
    )(scal, *got, *got, *caps, *caps, *spatial)
    back = [done[0]] + [lax.ppermute(done[s], "seq", crossed(s)) for s in (1, 2, 3)]
    block_spec = spec((FRAMES, 4 * PIXELS, HDIM), lambda h: (0, 0, h))
    solved = call(
        temporal_kernel,
        low(FRAMES, 4 * PIXELS, HALF),
        [SMEM, block_spec],
        block_spec,
        grid=(6,),
        flops=1_000_000,
        moved=10_000,
        name="temporal_attention",
        after=(back[1],),
    )(scal, block)
    returned = lax.all_to_all(
        solved, "seq", split_axis=0, concat_axis=0, tiled=True, axis_index_groups=GROUPS
    )
    sums = [c0] + [lax.ppermute(c, "seq", shifted(s, 0)) for s, c in ((1, c1), (2, c2), (3, c3))]
    both, spatial_grads, cross_query_grad = call(
        frame_unpack_kernel,
        [low(ROWS, WIDTH), low(3, ROWS, WIDTH), low(ROWS, WIDTH)],
        [SMEM] + [spec()] * 4,
        [spec()] * 3,
        flops=100_000_000_000,
        moved=4_000_000,
        name="frame_unpack",
    )(scal, *back)

    sums = call(
        cap_sum_y_kernel,
        [low(2, CAP_PAD, QUARTER)] * 4,
        [spec()] * 4,
        [spec()] * 4,
        moved=700_000,
        name="cap_sum_y",
        after=(both,),
        scratch=[pltpu.VMEM((2, 80, QUARTER), F32), pltpu.VMEM((2, CAP_PAD, QUARTER), F32)],
    )(*sums)
    sums = [sums[0]] + [lax.ppermute(sums[s], "seq", shifted(0, s)) for s in (1, 2, 3)]
    sums = call(
        cap_sum_z_kernel,
        [full(2, 8, QUARTER)] * 4,
        [spec()] * 4,
        [spec()] * 4,
        moved=300_000,
        name="cap_sum_z",
        scratch=[pltpu.VMEM((2, CAP_PAD, QUARTER), F32)],
    )(*sums)
    sums = [sums[0]] + [lax.ppermute(sums[s], "seq", crossed(s)) for s in (1, 2, 3)]
    sums = call(
        cap_place_kernel,
        full(2, 8, WIDTH),
        [SMEM] + [spec()] * 4,
        spec(),
        moved=200_000,
        name="cap_place",
    )(scal, *sums)
    caption_grads = jnp.swapaxes(sums[:, :5], 0, 1)
    steps = 4
    mixed, temporal_grads = call(
        temporal_unpack_kernel,
        [low(ROWS, WIDTH), low(3, ROWS, WIDTH)],
        [
            SMEM,
            spec((16 // steps, 4 * PIXELS, HALF), lambda i: (i, 0, 0)),
            spec((ROWS // steps, WIDTH), lambda i: (i, 0)),
        ],
        [
            spec((ROWS // steps, WIDTH), lambda i: (i, 0)),
            spec((3, ROWS // steps, WIDTH), lambda i: (0, i, 0)),
        ],
        grid=(steps,),
        moved=3_600_000,
        name="temporal_unpack",
    )(scal, returned, both)

    return (mixed, spatial_grads, temporal_grads, cross_query_grad, caption_grads)


def solution(mesh):
    placed = (
        P(None, ("dp", "seq"), None),
        P(None, ("dp", "seq"), None),
        P(("dp", "seq"), None),
        P(("dp", "seq"), None, None),
        P(("dp", "seq"), None),
        P("dp"),
        P("dp"),
    )
    return jax.shard_map(
        local,
        mesh=mesh,
        in_specs=placed,
        out_specs=(
            P(("dp", "seq"), None),
            P(None, ("dp", "seq"), None),
            P(None, ("dp", "seq"), None),
            P(("dp", "seq"), None),
            P(("dp", "seq"), None, None),
        ),
        check_vma=False,
    )
```

time: 541 us -> 159 us (0.29); the launches traced: 531 us -> 158 us
  waiting for transfers between devices: 322 us -> 75.2 us
  local copies, waits for them, and re-layouts: 74.8 us -> 5.51 us
  matrix products: 32.8 us -> 0 us
  Pallas kernels: 0 us -> 27.7 us
  other arithmetic: 24.3 us -> 0.16 us
  between operations: 17.1 us -> 2.07 us
  starting transfers between devices: 60.1 us -> 47 us
    unnamed x3 -> x0, waiting for transfers between devices: 168 us -> none
    all_to_all x8 -> x2, waiting for transfers between devices: 120 us -> 0.01 us  [the longest x1 0.01 us: local(): lax.all_to_all(solved, 'seq', split_axis=0, concat_axis=0, tiled=True, ax...]
    ppermute x4 -> x21, waiting for transfers between devices: 8.45 us -> 75.2 us  [the longest x3 28 us: local(): lax.ppermute(packs[s], 'seq', crossed(s))]
    all_to_all x8 -> x2, starting transfers between devices: 57.6 us -> 10.4 us  [the longest x1 5.38 us: local(): lax.all_to_all(solved, 'seq', split_axis=0, concat_axis=0, tiled=True, ax...]
    ppermute x4 -> x21, starting transfers between devices: 2.39 us -> 36.6 us  [the longest x3 11.3 us: local(): lax.ppermute(caption_kv, 'seq', shifted(0, -s))]
    pallas_call x0 -> x13, Pallas kernels: none -> 27.7 us  [the longest x12 27.7 us: call(): return lambda *args: made(*args, *after)]
    all_gather x1 -> x0, waiting for transfers between devices: 25.5 us -> none  [local(): caption_all = lax.all_gather(caption_kv, 'seq', axis=0, tiled=True)]
    dot_general x15 -> x0, matrix products: 24.4 us -> none  [the longest x3 6.45 us: attend_forward(): jnp.einsum('bhnm,bmhe->bnhe', weights_low, value_rows, preferred_element_...]
  transfers between devices with their start and end apart: 14 -> 23, of which waited for: 11 -> 10; matrix products, arithmetic and copies ran while one was open for 16% -> 0% of each run, Pallas kernels for 0% -> 15%
where the time goes in v1:
time: 159 us; the launch traced here: 158 us
  waiting for transfers between devices  75.2 us (47%)
  starting transfers between devices  47 us (30%)
  Pallas kernels  27.7 us (17%)
  local copies, waits for them, and re-layouts  5.51 us (3%)
  between operations  2.07 us (1%)
    ppermute x3, waiting for transfers between devices, local(): lax.ppermute(packs[s], 'seq', crossed(s))  28 us
    pallas_call x12, Pallas kernels, call(): return lambda *args: made(*args, *after)  27.7 us
    ppermute x3, waiting for transfers between devices, local(): lax.ppermute(done[s], 'seq', crossed(s))  20.4 us
    ppermute x3, waiting for transfers between devices, local(): lax.ppermute(sums[s], 'seq', shifted(0, s))  15.5 us
    ppermute x3, starting transfers between devices, local(): lax.ppermute(caption_kv, 'seq', shifted(0, -s))  11.3 us
    ppermute x3, waiting for transfers between devices, local(): lax.ppermute(caps, 'seq', shifted(-s, 0))  8.99 us
    ppermute x3, starting transfers between devices, local(): lax.ppermute(sums[s], 'seq', shifted(0, s))  7.8 us
    ppermute x3, starting transfers between devices, local(): lax.ppermute(caps, 'seq', shifted(-s, 0))  5.9 us
  transfers between devices with their start and end apart: 23, of which 10 were waited for; matrix products, arithmetic and copies ran while one was open for 0% of the time, Pallas kernels for 15%

profile of v1, /device:TPU:2, one launch (start us, length us, event | category | flops | bytes accessed | tf_op | source)
XLA Modules:
  0.0 157.7 jit_solution(11493715145715858262)
XLA Ops:
  1.4 3.3 %collective-permute-start.2 = (bf16[5,2,1536]{2,0,1:T(8,128)(2,1)S(1)}, bf16[5,2,1536]{2,0,1:T(8,128)(2,1)S(1)}, u32[]{:S(2)}, u32[]{:S(2)}) collective-permute-start(bf16[5,2,1536]{2,0,1:T(8,128)(2,1)S(1)} %copy.24), channel_id=1, source_target_pairs={{0,4},{1,5},{2,6},{3,7},{4,8},{5,9},{6,10},{7,11},{8,12},{9,13},{1... | collective-permute-start | bytes 92168 | tf_op jit(solution)/shard_map/ppermute | solution.py:306
  4.7 5.4 %collective-permute-start.1 = (bf16[5,2,1536]{2,0,1:T(8,128)(2,1)S(1)}, bf16[5,2,1536]{2,0,1:T(8,128)(2,1)S(1)}, u32[]{:S(2)}, u32[]{:S(2)}) collective-permute-start(bf16[5,2,1536]{2,0,1:T(8,128)(2,1)S(1)} %copy.24), channel_id=1, source_target_pairs={{0,8},{1,9},{2,10},{3,11},{4,12},{5,13},{6,14},{7,15},{8,0},{9,1},... | collective-permute-start | bytes 92168 | tf_op jit(solution)/shard_map/ppermute | solution.py:306
  10.1 2.7 %collective-permute-start = (bf16[5,2,1536]{2,0,1:T(8,128)(2,1)S(1)}, bf16[5,2,1536]{2,0,1:T(8,128)(2,1)S(1)}, u32[]{:S(2)}, u32[]{:S(2)}) collective-permute-start(bf16[5,2,1536]{2,0,1:T(8,128)(2,1)S(1)} %copy.24), channel_id=1, source_target_pairs={{0,12},{1,13},{2,14},{3,15},{4,0},{5,1},{6,2},{7,3},{8,4},{9,5},{1... | collective-permute-start | bytes 92168 | tf_op jit(solution)/shard_map/ppermute | solution.py:306
  23.6 5.0 %all-to-all-start = ((bf16[16,64,768]{2,1,0:T(8,128)(2,1)}), bf16[16,64,768]{2,1,0:T(8,128)(2,1)S(1)}, u32[]{:S(2)}, u32[]{:S(2)}) async-start(bf16[16,64,768]{2,1,0:T(8,128)(2,1)} %gate.1), calls=%async_computation | async-start | bytes 3145728 | tf_op jit(solution)/shard_map/all_to_all | solution.py:343
  28.6 16.8 %collective-permute-done.4.refs_3_.refs_2_.refs_7_ = bf16[704,384]{1,0:T(8,128)(2,1)S(1)} collective-permute-done((bf16[704,384]{1,0:T(8,128)(2,1)}, bf16[704,384]{1,0:T(8,128)(2,1)S(1)}, u32[]{:S(2)}, u32[]{:S(2)}) %collective-permute-start.4) | collective-permute-done | bytes 540704 | tf_op jit(solution)/shard_map/ppermute | solution.py:340
  45.4 11.2 %collective-permute-done.5.refs_4_.refs_3_.refs_8_ = bf16[704,384]{1,0:T(8,128)(2,1)} collective-permute-done((bf16[704,384]{1,0:T(8,128)(2,1)}, bf16[704,384]{1,0:T(8,128)(2,1)}, u32[]{:S(2)}, u32[]{:S(2)}) %collective-permute-start.5) | collective-permute-done | bytes 540704 | tf_op jit(solution)/shard_map/ppermute | solution.py:340
  56.6 6.3 %spatial_attention.1 = (bf16[640,384]{1,0:T(8,128)(2,1)S(1)}, bf16[640,384]{1,0:T(8,128)(2,1)S(1)}, bf16[640,384]{1,0:T(8,128)(2,1)}, bf16[640,384]{1,0:T(8,128)(2,1)}) custom-call(s32[4]{0:T(128)S(1)} %pad_add_fusion.refs_0_, bf16[704,384]{1,0:T(8,128)(2,1)S(1)} %get-tuple-element.42.refs_1_.refs_0_.refs_5_, ...), custom_call_target="tpu_custom_call" | custom-call | flops 99999997952 | bytes 4000000 | tf_op jit(solution)/shard_map/spatial_attention/pallas_call | solution.py:255
  65.5 2.9 %collective-permute-start.7 = (bf16[80,768]{1,0:T(8,128)(2,1)S(1)}, bf16[80,768]{1,0:T(8,128)(2,1)S(1)}, u32[]{:S(2)}, u32[]{:S(2)}) collective-permute-start(bf16[80,768]{1,0:T(8,128)(2,1)S(1)} %cap_join.1.refs_9_.refs_13_), channel_id=1, source_target_pairs={{0,32},{1,33},{2,34},{3,35},{4,36},{5,37},{6,38},{7,39},{8,40},{9,... | collective-permute-start | bytes 368648 | tf_op jit(solution)/shard_map/ppermute | solution.py:371
  69.7 2.9 %collective-permute-done.8.refs_12_.refs_16_ = bf16[80,768]{1,0:T(8,128)(2,1)S(1)} collective-permute-done((bf16[80,768]{1,0:T(8,128)(2,1)S(1)}, bf16[80,768]{1,0:T(8,128)(2,1)S(1)}, u32[]{:S(2)}, u32[]{:S(2)}) %collective-permute-start.8) | collective-permute-done | bytes 122912 | tf_op jit(solution)/shard_map/ppermute | solution.py:371
  72.6 5.5 %collective-permute-done.7.refs_11_.refs_15_ = bf16[80,768]{1,0:T(8,128)(2,1)S(1)} collective-permute-done((bf16[80,768]{1,0:T(8,128)(2,1)S(1)}, bf16[80,768]{1,0:T(8,128)(2,1)S(1)}, u32[]{:S(2)}, u32[]{:S(2)}) %collective-permute-start.7) | collective-permute-done | bytes 122912 | tf_op jit(solution)/shard_map/ppermute | solution.py:371
  78.7 5.3 %cross_attention.1 = (bf16[640,384]{1,0:T(8,128)(2,1)S(1)}, bf16[640,384]{1,0:T(8,128)(2,1)S(1)}, bf16[640,384]{1,0:T(8,128)(2,1)}, bf16[640,384]{1,0:T(8,128)(2...) custom-call(s32[4]{0:T(128)S(1)} %pad_add_fusion.refs_0_, ...), custom_call_target="tpu_custom_call", output_to_operand_aliasing={{0}: (17, {}), {1}: (18, {}), {2}: (19, {}), {3}: (20, {})} | custom-call | flops 1000000000 | bytes 3000000 | tf_op jit(solution)/shard_map/cross_attention/pallas_call | solution.py:255
  84.9 1.9 %collective-permute-start.10 = (bf16[640,384]{1,0:T(8,128)(2,1)}, bf16[640,384]{1,0:T(8,128)(2,1)}, u32[]{:S(2)}, u32[]{:S(2)}) collective-permute-start(bf16[640,384]{1,0:T(8,128)(2,1)} %get-tuple-element.52), channel_id=1, source_target_pairs={{0,2},{1,3},{2,0},{3,1},{4,6},{5,7},{6,4},{7,5},{8,10},{9,11},{10,... | collective-permute-start | bytes 1474568 | tf_op jit(solution)/shard_map/ppermute | solution.py:390
  86.8 2.0 %collective-permute-start.12 = (bf16[2,80,384]{2,1,0:T(8,128)(2,1)}, bf16[2,80,384]{2,1,0:T(8,128)(2,1)S(1)}, u32[]{:S(2)}, u32[]{:S(2)}) collective-permute-start(bf16[2,80,384]{2,1,0:T(8,128)(2,1)} %get-tuple-element.60), channel_id=1, source_target_pairs={{0,16},{1,17},{2,18},{3,19},{4,20},{5,21},{6,22},{7,23},{8,24},{9,... | collective-permute-start | bytes 368648 | tf_op jit(solution)/shard_map/ppermute | solution.py:406
  88.8 2.3 %collective-permute-start.13 = (bf16[2,80,384]{2,1,0:T(8,128)(2,1)}, bf16[2,80,384]{2,1,0:T(8,128)(2,1)S(1)}, u32[]{:S(2)}, u32[]{:S(2)}) collective-permute-start(bf16[2,80,384]{2,1,0:T(8,128)(2,1)} %get-tuple-element.61), channel_id=1, source_target_pairs={{0,32},{1,33},{2,34},{3,35},{4,36},{5,37},{6,38},{7,39},{8,40},{9,... | collective-permute-start | bytes 368648 | tf_op jit(solution)/shard_map/ppermute | solution.py:406
  92.5 5.6 %temporal_attention.1 = bf16[16,64,768]{2,1,0:T(8,128)(2,1)} custom-call(s32[4]{0:T(128)S(1)} %pad_add_fusion.refs_0_, bf16[16,64,768]{2,1,0:T(8,128)(2,1)S(1)} %all-to-all-done.refs_1_, bf16[640,384]{1,0:T(8,128)(2,1)S(1)} %collective-permute-done.9.refs_2_), custom_call_target="tpu_custom_call" | custom-call | flops 1000000 | bytes 10000 | tf_op jit(solution)/shard_map/temporal_attention/pallas_call | solution.py:255
  98.1 5.4 %all-to-all-start.1 = ((bf16[16,64,768]{2,1,0:T(8,128)(2,1)}), bf16[16,64,768]{2,1,0:T(8,128)(2,1)S(1)}, u32[]{:S(2)}, u32[]{:S(2)}) async-start(bf16[16,64,768]{2,1,0:T(8,128)(2,1)} %temporal_attention.1), calls=%async_computation.1 | async-start | bytes 3145728 | tf_op jit(solution)/shard_map/all_to_all | solution.py:403
  103.5 20.4 %collective-permute-done.11.refs_4_ = bf16[640,384]{1,0:T(8,128)(2,1)} collective-permute-done((bf16[640,384]{1,0:T(8,128)(2,1)}, bf16[640,384]{1,0:T(8,128)(2,1)}, u32[]{:S(2)}, u32[]{:S(2)}) %collective-permute-start.11) | collective-permute-done | bytes 491552 | tf_op jit(solution)/shard_map/ppermute | solution.py:390
  123.9 2.5 %frame_unpack.1 = (bf16[128,1536]{1,0:T(8,128)(2,1)S(1)}, bf16[3,128,1536]{2,1,0:T(8,128)(2,1)}, bf16[128,1536]{1,0:T(8,128)(2,1)}) custom-call(s32[4]{0:T(128)S(1)} %pad_add_fusion.refs_0_, bf16[640,384]{1,0:T(8,128)(2,1)S(1)} %copy-done.1, bf16[640,384]{1,0:T(8,128)(2,1)S(1)} %collective-permute-done.9.refs_2_, ...), custom_call_target="tpu_custom_call" | custom-call | flops 99999997952 | bytes 4000000 | tf_op jit(solution)/shard_map/frame_unpack/pallas_call | solution.py:255
  126.7 3.7 %collective-permute-start.16 = (bf16[2,32,384]{2,1,0:T(8,128)(2,1)S(1)}, bf16[2,32,384]{2,1,0:T(8,128)(2,1)S(1)}, u32[]{:S(2)}, u32[]{:S(2)}) collective-permute-start(bf16[2,32,384]{2,1,0:T(8,128)(2,1)S(1)} %get-tuple-element.65), channel_id=1, source_target_pairs={{0,8},{1,9},{2,10},{3,11},{4,12},{5,13},{6,14},{7,15},{8,0},{9,1},... | collective-permute-start | bytes 147464 | tf_op jit(solution)/shard_map/ppermute | solution.py:427
  130.3 4.0 %collective-permute-start.17 = (bf16[2,32,384]{2,1,0:T(8,128)(2,1)S(1)}, bf16[2,32,384]{2,1,0:T(8,128)(2,1)S(1)}, u32[]{:S(2)}, u32[]{:S(2)}) collective-permute-start(bf16[2,32,384]{2,1,0:T(8,128)(2,1)S(1)} %get-tuple-element.66), channel_id=1, source_target_pairs={{0,12},{1,13},{2,14},{3,15},{4,0},{5,1},{6,2},{7,3},{8,4},{9,5},{1... | collective-permute-start | bytes 147464 | tf_op jit(solution)/shard_map/ppermute | solution.py:427
  134.4 11.6 %collective-permute-done.15.refs_1_ = bf16[2,32,384]{2,1,0:T(8,128)(2,1)S(1)} collective-permute-done((bf16[2,32,384]{2,1,0:T(8,128)(2,1)S(1)}, bf16[2,32,384]{2,1,0:T(8,128)(2,1)S(1)}, u32[]{:S(2)}, u32[]{:S(2)}) %collective-permute-start.15) | collective-permute-done | bytes 49184 | tf_op jit(solution)/shard_map/ppermute | solution.py:427
  146.0 3.9 %collective-permute-done.16.refs_2_ = bf16[2,32,384]{2,1,0:T(8,128)(2,1)S(1)} collective-permute-done((bf16[2,32,384]{2,1,0:T(8,128)(2,1)S(1)}, bf16[2,32,384]{2,1,0:T(8,128)(2,1)S(1)}, u32[]{:S(2)}, u32[]{:S(2)}) %collective-permute-start.16) | collective-permute-done | bytes 49184 | tf_op jit(solution)/shard_map/ppermute | solution.py:427
  151.9 2.1 %collective-permute-done.19.refs_3_ = f32[2,8,384]{2,1,0:T(8,128)S(1)} collective-permute-done((f32[2,8,384]{2,1,0:T(8,128)S(1)}, f32[2,8,384]{2,1,0:T(8,128)S(1)}, u32[]{:S(2)}, u32[]{:S(2)}) %collective-permute-start.19) | collective-permute-done | bytes 24608 | tf_op jit(solution)/shard_map/ppermute | solution.py:437
  155.4 2.2 %temporal_unpack.1 = (bf16[128,1536]{1,0:T(8,128)(2,1)}, bf16[3,128,1536]{2,1,0:T(8,128)(2,1)}) custom-call(s32[4]{0:T(128)S(1)} %pad_add_fusion.refs_0_, bf16[16,64,768]{2,1,0:T(8,128)(2,1)S(1)} %all-to-all-done.1.refs_1_, bf16[128,1536]{1,0:T(8,128)(2,1)S(1)} %get-tuple-element.54.refs_2_.refs_4_), custom_call_target="tpu_custom_call" | custom-call | bytes 3600000 | tf_op jit(solution)/shard_map/temporal_unpack/pallas_call | solution.py:255
  (55 shorter events, 20.9 us)
Async XLA Ops:
  1.4 19.0 %collective-permute-start.2 = (bf16[5,2,1536]{2,0,1:T(8,128)(2,1)S(1)}, bf16[5,2,1536]{2,0,1:T(8,128)(2,1)S(1)}, u32[]{:S(2)}, u32[]{:S(2)}) collective-permute-start(bf16[5,2,1536]{2,0,1:T(8,128)(2,1)S(1)} %copy.24), channel_id=1, source_target_pairs={{0,4},{1,5},{2,6},{3,7},{4,8},{5,9},{6,10},{7,11},{8,12},{9,13},{1... | collective-permute-start | bytes 92168 | tf_op jit(solution)/shard_map/ppermute | solution.py:306
  4.7 15.7 %collective-permute-start.1 = (bf16[5,2,1536]{2,0,1:T(8,128)(2,1)S(1)}, bf16[5,2,1536]{2,0,1:T(8,128)(2,1)S(1)}, u32[]{:S(2)}, u32[]{:S(2)}) collective-permute-start(bf16[5,2,1536]{2,0,1:T(8,128)(2,1)S(1)} %copy.24), channel_id=1, source_target_pairs={{0,8},{1,9},{2,10},{3,11},{4,12},{5,13},{6,14},{7,15},{8,0},{9,1},... | collective-permute-start | bytes 92168 | tf_op jit(solution)/shard_map/ppermute | solution.py:306
  10.1 10.3 %collective-permute-start = (bf16[5,2,1536]{2,0,1:T(8,128)(2,1)S(1)}, bf16[5,2,1536]{2,0,1:T(8,128)(2,1)S(1)}, u32[]{:S(2)}, u32[]{:S(2)}) collective-permute-start(bf16[5,2,1536]{2,0,1:T(8,128)(2,1)S(1)} %copy.24), channel_id=1, source_target_pairs={{0,12},{1,13},{2,14},{3,15},{4,0},{5,1},{6,2},{7,3},{8,4},{9,5},{1... | collective-permute-start | bytes 92168 | tf_op jit(solution)/shard_map/ppermute | solution.py:306
  21.7 6.9 %collective-permute-start.3 = (bf16[704,384]{1,0:T(8,128)(2,1)}, bf16[704,384]{1,0:T(8,128)(2,1)S(1)}, u32[]{:S(2)}, u32[]{:S(2)}) collective-permute-start(bf16[704,384]{1,0:T(8,128)(2,1)} %get-tuple-element.43), channel_id=1, source_target_pairs={{0,1},{1,0},{2,3},{3,2},{4,5},{5,4},{6,7},{7,6},{8,9},{9,8},{10,11... | collective-permute-start | bytes 1622024 | tf_op jit(solution)/shard_map/ppermute | solution.py:340
  21.7 23.7 %collective-permute-start.4 = (bf16[704,384]{1,0:T(8,128)(2,1)}, bf16[704,384]{1,0:T(8,128)(2,1)S(1)}, u32[]{:S(2)}, u32[]{:S(2)}) collective-permute-start(bf16[704,384]{1,0:T(8,128)(2,1)} %get-tuple-element.44), channel_id=1, source_target_pairs={{0,2},{1,3},{2,0},{3,1},{4,6},{5,7},{6,4},{7,5},{8,10},{9,11},{10,... | collective-permute-start | bytes 1622024 | tf_op jit(solution)/shard_map/ppermute | solution.py:340
  22.7 33.9 %collective-permute-start.5 = (bf16[704,384]{1,0:T(8,128)(2,1)}, bf16[704,384]{1,0:T(8,128)(2,1)}, u32[]{:S(2)}, u32[]{:S(2)}) collective-permute-start(bf16[704,384]{1,0:T(8,128)(2,1)} %get-tuple-element.45), channel_id=1, source_target_pairs={{0,3},{1,2},{2,1},{3,0},{4,7},{5,6},{6,5},{7,4},{8,11},{9,10},{10,... | collective-permute-start | bytes 1622024 | tf_op jit(solution)/shard_map/ppermute | solution.py:340
  23.6 68.9 %all-to-all-start = ((bf16[16,64,768]{2,1,0:T(8,128)(2,1)}), bf16[16,64,768]{2,1,0:T(8,128)(2,1)S(1)}, u32[]{:S(2)}, u32[]{:S(2)}) async-start(bf16[16,64,768]{2,1,0:T(8,128)(2,1)} %gate.1), calls=%async_computation | async-start | bytes 3145728 | tf_op jit(solution)/shard_map/all_to_all | solution.py:343
  63.8 8.8 %collective-permute-start.8 = (bf16[80,768]{1,0:T(8,128)(2,1)S(1)}, bf16[80,768]{1,0:T(8,128)(2,1)S(1)}, u32[]{:S(2)}, u32[]{:S(2)}) collective-permute-start(bf16[80,768]{1,0:T(8,128)(2,1)S(1)} %cap_join.1.refs_9_.refs_13_), channel_id=1, source_target_pairs={{0,16},{1,17},{2,18},{3,19},{4,20},{5,21},{6,22},{7,23},{8,24},{9,... | collective-permute-start | bytes 368648 | tf_op jit(solution)/shard_map/ppermute | solution.py:371
  65.5 12.6 %collective-permute-start.7 = (bf16[80,768]{1,0:T(8,128)(2,1)S(1)}, bf16[80,768]{1,0:T(8,128)(2,1)S(1)}, u32[]{:S(2)}, u32[]{:S(2)}) collective-permute-start(bf16[80,768]{1,0:T(8,128)(2,1)S(1)} %cap_join.1.refs_9_.refs_13_), channel_id=1, source_target_pairs={{0,32},{1,33},{2,34},{3,35},{4,36},{5,37},{6,38},{7,39},{8,40},{9,... | collective-permute-start | bytes 368648 | tf_op jit(solution)/shard_map/ppermute | solution.py:371
  68.4 10.3 %collective-permute-start.6 = (bf16[80,768]{1,0:T(8,128)(2,1)S(1)}, bf16[80,768]{1,0:T(8,128)(2,1)S(1)}, u32[]{:S(2)}, u32[]{:S(2)}) collective-permute-start(bf16[80,768]{1,0:T(8,128)(2,1)S(1)} %cap_join.1.refs_9_.refs_13_), channel_id=1, source_target_pairs={{0,48},{1,49},{2,50},{3,51},{4,52},{5,53},{6,54},{7,55},{8,56},{9,... | collective-permute-start | bytes 368648 | tf_op jit(solution)/shard_map/ppermute | solution.py:371
  84.7 6.3 %collective-permute-start.9 = (bf16[640,384]{1,0:T(8,128)(2,1)S(1)}, bf16[640,384]{1,0:T(8,128)(2,1)S(1)}, u32[]{:S(2)}, u32[]{:S(2)}) collective-permute-start(bf16[640,384]{1,0:T(8,128)(2,1)S(1)} %get-tuple-element.50), channel_id=1, source_target_pairs={{0,1},{1,0},{2,3},{3,2},{4,5},{5,4},{6,7},{7,6},{8,9},{9,8},{10,11... | collective-permute-start | bytes 1474568 | tf_op jit(solution)/shard_map/ppermute | solution.py:390
  84.9 18.6 %collective-permute-start.10 = (bf16[640,384]{1,0:T(8,128)(2,1)}, bf16[640,384]{1,0:T(8,128)(2,1)}, u32[]{:S(2)}, u32[]{:S(2)}) collective-permute-start(bf16[640,384]{1,0:T(8,128)(2,1)} %get-tuple-element.52), channel_id=1, source_target_pairs={{0,2},{1,3},{2,0},{3,1},{4,6},{5,7},{6,4},{7,5},{8,10},{9,11},{10,... | collective-permute-start | bytes 1474568 | tf_op jit(solution)/shard_map/ppermute | solution.py:390
  86.8 37.2 %collective-permute-start.11 = (bf16[640,384]{1,0:T(8,128)(2,1)}, bf16[640,384]{1,0:T(8,128)(2,1)}, u32[]{:S(2)}, u32[]{:S(2)}) collective-permute-start(bf16[640,384]{1,0:T(8,128)(2,1)} %get-tuple-element.53), channel_id=1, source_target_pairs={{0,3},{1,2},{2,1},{3,0},{4,7},{5,6},{6,5},{7,4},{8,11},{9,10},{10,... | collective-permute-start | bytes 1474568 | tf_op jit(solution)/shard_map/ppermute | solution.py:390
  86.8 39.6 %collective-permute-start.12 = (bf16[2,80,384]{2,1,0:T(8,128)(2,1)}, bf16[2,80,384]{2,1,0:T(8,128)(2,1)S(1)}, u32[]{:S(2)}, u32[]{:S(2)}) collective-permute-start(bf16[2,80,384]{2,1,0:T(8,128)(2,1)} %get-tuple-element.60), channel_id=1, source_target_pairs={{0,16},{1,17},{2,18},{3,19},{4,20},{5,21},{6,22},{7,23},{8,24},{9,... | collective-permute-start | bytes 368648 | tf_op jit(solution)/shard_map/ppermute | solution.py:406
  88.8 37.6 %collective-permute-start.13 = (bf16[2,80,384]{2,1,0:T(8,128)(2,1)}, bf16[2,80,384]{2,1,0:T(8,128)(2,1)S(1)}, u32[]{:S(2)}, u32[]{:S(2)}) collective-permute-start(bf16[2,80,384]{2,1,0:T(8,128)(2,1)} %get-tuple-element.61), channel_id=1, source_target_pairs={{0,32},{1,33},{2,34},{3,35},{4,36},{5,37},{6,38},{7,39},{8,40},{9,... | collective-permute-start | bytes 368648 | tf_op jit(solution)/shard_map/ppermute | solution.py:406
  91.1 35.3 %collective-permute-start.14 = (bf16[2,80,384]{2,1,0:T(8,128)(2,1)}, bf16[2,80,384]{2,1,0:T(8,128)(2,1)S(1)}, u32[]{:S(2)}, u32[]{:S(2)}) collective-permute-start(bf16[2,80,384]{2,1,0:T(8,128)(2,1)} %get-tuple-element.62), channel_id=1, source_target_pairs={{0,48},{1,49},{2,50},{3,51},{4,52},{5,53},{6,54},{7,55},{8,56},{9,... | collective-permute-start | bytes 368648 | tf_op jit(solution)/shard_map/ppermute | solution.py:406
  98.1 25.8 %copy-start.1 = (bf16[640,384]{1,0:T(8,128)(2,1)S(1)}, bf16[640,384]{1,0:T(8,128)(2,1)}, u32[]{:S(2)}) copy-start(bf16[640,384]{1,0:T(8,128)(2,1)} %copy-done) | copy-start | bytes 1474564
  98.1 57.3 %all-to-all-start.1 = ((bf16[16,64,768]{2,1,0:T(8,128)(2,1)}), bf16[16,64,768]{2,1,0:T(8,128)(2,1)S(1)}, u32[]{:S(2)}, u32[]{:S(2)}) async-start(bf16[16,64,768]{2,1,0:T(8,128)(2,1)} %temporal_attention.1), calls=%async_computation.1 | async-start | bytes 3145728 | tf_op jit(solution)/shard_map/all_to_all | solution.py:403
  126.6 19.4 %collective-permute-start.15 = (bf16[2,32,384]{2,1,0:T(8,128)(2,1)S(1)}, bf16[2,32,384]{2,1,0:T(8,128)(2,1)S(1)}, u32[]{:S(2)}, u32[]{:S(2)}) collective-permute-start(bf16[2,32,384]{2,1,0:T(8,128)(2,1)S(1)} %get-tuple-element.64), channel_id=1, source_target_pairs={{0,4},{1,5},{2,6},{3,7},{4,8},{5,9},{6,10},{7,11},{8,12},{9,13},{1... | collective-permute-start | bytes 147464 | tf_op jit(solution)/shard_map/ppermute | solution.py:427
  126.7 23.2 %collective-permute-start.16 = (bf16[2,32,384]{2,1,0:T(8,128)(2,1)S(1)}, bf16[2,32,384]{2,1,0:T(8,128)(2,1)S(1)}, u32[]{:S(2)}, u32[]{:S(2)}) collective-permute-start(bf16[2,32,384]{2,1,0:T(8,128)(2,1)S(1)} %get-tuple-element.65), channel_id=1, source_target_pairs={{0,8},{1,9},{2,10},{3,11},{4,12},{5,13},{6,14},{7,15},{8,0},{9,1},... | collective-permute-start | bytes 147464 | tf_op jit(solution)/shard_map/ppermute | solution.py:427
  130.3 19.5 %collective-permute-start.17 = (bf16[2,32,384]{2,1,0:T(8,128)(2,1)S(1)}, bf16[2,32,384]{2,1,0:T(8,128)(2,1)S(1)}, u32[]{:S(2)}, u32[]{:S(2)}) collective-permute-start(bf16[2,32,384]{2,1,0:T(8,128)(2,1)S(1)} %get-tuple-element.66), channel_id=1, source_target_pairs={{0,12},{1,13},{2,14},{3,15},{4,0},{5,1},{6,2},{7,3},{8,4},{9,5},{1... | collective-permute-start | bytes 147464 | tf_op jit(solution)/shard_map/ppermute | solution.py:427
  149.9 2.0 %collective-permute-start.18 = (f32[2,8,384]{2,1,0:T(8,128)S(1)}, f32[2,8,384]{2,1,0:T(8,128)S(1)}, u32[]{:S(2)}, u32[]{:S(2)}) collective-permute-start(f32[2,8,384]{2,1,0:T(8,128)S(1)} %get-tuple-element.68), channel_id=1, source_target_pairs={{0,1},{1,0},{2,3},{3,2},{4,5},{5,4},{6,7},{7,6},{8,9},{9,8},{10,11... | collective-permute-start | bytes 73736 | tf_op jit(solution)/shard_map/ppermute | solution.py:437
  150.0 3.9 %collective-permute-start.19 = (f32[2,8,384]{2,1,0:T(8,128)S(1)}, f32[2,8,384]{2,1,0:T(8,128)S(1)}, u32[]{:S(2)}, u32[]{:S(2)}) collective-permute-start(f32[2,8,384]{2,1,0:T(8,128)S(1)} %get-tuple-element.69), channel_id=1, source_target_pairs={{0,2},{1,3},{2,0},{3,1},{4,6},{5,7},{6,4},{7,5},{8,10},{9,11},{10,... | collective-permute-start | bytes 73736 | tf_op jit(solution)/shard_map/ppermute | solution.py:437
  150.9 3.3 %collective-permute-start.20 = (f32[2,8,384]{2,1,0:T(8,128)S(1)}, f32[2,8,384]{2,1,0:T(8,128)S(1)}, u32[]{:S(2)}, u32[]{:S(2)}) collective-permute-start(f32[2,8,384]{2,1,0:T(8,128)S(1)} %get-tuple-element.70), channel_id=1, source_target_pairs={{0,3},{1,2},{2,1},{3,0},{4,7},{5,6},{6,5},{7,4},{8,11},{9,10},{10,... | collective-permute-start | bytes 73736 | tf_op jit(solution)/shard_map/ppermute | solution.py:437
  (6 other events, 7.5 us)

commit v2 on v1

--- a/solution.py
+++ b/solution.py
@@ -103,12 +103,16 @@
         put_rows(outs, i + 2, item)
 
 
-def cap_pack_kernel(scal, caps, m0, m1, m2, m3, *outs):
-    for step, out in enumerate(outs):
+def cap_pack_kernel(scal, p0, p1, p2, p3, m0, m1, m2, m3, o0, o1, o2, o3, rows):
+    rows[...] = jnp.zeros_like(rows)
+    for i, part in enumerate((p0, p1, p2, p3)):
+        for kind in range(2):
+            first = kind * CAP_PAD + 5 * i
+            rows[first : first + 5, :] = part[kind].astype(F32)
+    for step, out in enumerate((o0, o1, o2, o3)):
         block = jnp.bitwise_xor(scal[0], step)
         lanes = pl.ds(pl.multiple_of(block * QUARTER, 128), QUARTER)
-        for kind in range(2):
-            out[kind * CAP_PAD : (kind + 1) * CAP_PAD, :] = caps[kind, :, lanes]
+        out[...] = rows[:, lanes].astype(BF16)
 
 
 def cap_join_kernel(m0, m1, m2, m3, out, rows):
@@ -255,21 +259,6 @@
     return lambda *args: made(*args, *after)
 
 
-def gate(arrays, after):
-    anywhere = pl.BlockSpec(memory_space=pl.ANY)
-    count = len(arrays)
-    return pl.pallas_call(
-        lambda *refs: None,
-        out_shape=[jax.ShapeDtypeStruct(a.shape, a.dtype) for a in arrays],
-        in_specs=[anywhere] * (count + len(after)),
-        out_specs=[anywhere] * count,
-        input_output_aliases={i: i for i in range(count)},
-        compiler_params=pltpu.CompilerParams(vmem_limit_bytes=VMEM_LIMIT),
-        cost_estimate=pl.CostEstimate(flops=0, bytes_accessed=1000, transcendentals=0),
-        name="gate",
-    )(*arrays, *after)
-
-
 def low(*shape):
     return jax.ShapeDtypeStruct(shape, BF16)
 
@@ -302,8 +291,6 @@
     index = lax.axis_index("seq").astype(jnp.int32)
     me, frame = index % 4, index // 4
     scal = jnp.stack([me, frame, live_tokens[0], caption_len[0]])
-
-    caps = [caption_kv] + [lax.ppermute(caption_kv, "seq", shifted(0, -s)) for s in (1, 2, 3)]
 
     packs = call(
         frame_pack_kernel,
@@ -314,6 +301,22 @@
         moved=1000,
         name="frame_pack",
     )(scal, spatial_qkv, out_grad, cross_query)
+    caps = jnp.swapaxes(caption_kv, 0, 1)
+    caps = [caps] + [lax.ppermute(caps, "seq", shifted(0, -s)) for s in (1, 2, 3)]
+    cap_rows = spec((2 * CAP_PAD, QUARTER), lambda i: (5 * ROWS // (2 * CAP_PAD), 0))
+    packs = call(
+        cap_pack_kernel,
+        [low(MESSAGE, QUARTER)] * 4,
+        [SMEM] + [spec()] * 4 + [pl.BlockSpec(memory_space=pl.ANY)] * 4,
+        [cap_rows] * 4,
+        grid=(1,),
+        moved=1000,
+        name="cap_pack",
+        aliases={5 + i: i for i in range(4)},
+        scratch=[pltpu.VMEM((2 * CAP_PAD, WIDTH), F32)],
+    )(scal, *caps, *packs)
+    got = [packs[0]] + [lax.ppermute(packs[s], "seq", crossed(s)) for s in (1, 2, 3)]
+
     sent = call(
         temporal_pack_kernel,
         low(16, 4 * PIXELS, HALF),
@@ -323,23 +326,6 @@
         name="temporal_pack",
         after=(packs[0],),
     )(temporal_qkv, out_grad)
-    caps = jnp.swapaxes(jnp.concatenate(caps, axis=0), 0, 1)
-    caps = jnp.pad(caps, ((0, 0), (0, CAP_PAD - 20), (0, 0)))
-    cap_rows = spec((2 * CAP_PAD, QUARTER), lambda i: (5 * ROWS // (2 * CAP_PAD), 0))
-    packs = call(
-        cap_pack_kernel,
-        [low(MESSAGE, QUARTER)] * 4,
-        [SMEM, spec()] + [pl.BlockSpec(memory_space=pl.ANY)] * 4,
-        [cap_rows] * 4,
-        grid=(1,),
-        moved=1000,
-        name="cap_pack",
-        after=(sent,),
-        aliases={2 + i: i for i in range(4)},
-    )(scal, caps, *packs)
-    got = [packs[0]] + [lax.ppermute(packs[s], "seq", crossed(s)) for s in (1, 2, 3)]
-
-    (sent,) = gate([sent], [packs[0]])
     block = lax.all_to_all(
         sent, "seq", split_axis=0, concat_axis=0, tiled=True, axis_index_groups=GROUPS
     )
@@ -365,7 +351,6 @@
         grid=(1,),
         moved=300_000,
         name="cap_join",
-        after=(spatial[0],),
         scratch=[pltpu.VMEM((80, HALF), F32)],
     )(*got)
     caps = [caps] + [lax.ppermute(caps, "seq", shifted(-s, 0)) for s in (1, 2, 3)]
@@ -412,6 +397,7 @@
         flops=100_000_000_000,
         moved=4_000_000,
         name="frame_unpack",
+        after=(solved,),
     )(scal, *back)
 
     sums = call(
@@ -435,15 +421,6 @@
         scratch=[pltpu.VMEM((2, CAP_PAD, QUARTER), F32)],
     )(*sums)
     sums = [sums[0]] + [lax.ppermute(sums[s], "seq", crossed(s)) for s in (1, 2, 3)]
-    sums = call(
-        cap_place_kernel,
-        full(2, 8, WIDTH),
-        [SMEM] + [spec()] * 4,
-        spec(),
-        moved=200_000,
-        name="cap_place",
-    )(scal, *sums)
-    caption_grads = jnp.swapaxes(sums[:, :5], 0, 1)
     steps = 4
     mixed, temporal_grads = call(
         temporal_unpack_kernel,
@@ -462,6 +439,16 @@
         name="temporal_unpack",
     )(scal, returned, both)
 
+    sums = call(
+        cap_place_kernel,
+        full(2, 8, WIDTH),
+        [SMEM] + [spec()] * 4,
+        spec(),
+        moved=200_000,
+        name="cap_place",
+        after=(mixed,),
+    )(scal, *sums)
+    caption_grads = jnp.swapaxes(sums[:, :5], 0, 1)
     return (mixed, spatial_grads, temporal_grads, cross_query_grad, caption_grads)
 
 

time: 159 us -> 150 us (0.943)
  waiting for transfers between devices: 75.2 us -> 56.8 us
  starting transfers between devices: 47 us -> 52.5 us
  local copies, waits for them, and re-layouts: 5.51 us -> 9.08 us
    ppermute x3, waiting for transfers between devices: 8.99 us -> 1.71 us  [local(): lax.ppermute(caps, 'seq', shifted(-s, 0))]
    ppermute x3, waiting for transfers between devices: 20.4 us -> 13.6 us  [local(): lax.ppermute(done[s], 'seq', crossed(s))]
    ppermute x3, starting transfers between devices: 7.8 us -> 13.1 us  [local(): lax.ppermute(sums[s], 'seq', shifted(0, s))]
    unnamed x16 -> x20, local copies, waits for them, and re-layouts: 5.48 us -> 9.07 us
    ppermute x3, waiting for transfers between devices: 28 us -> 24.8 us  [local(): lax.ppermute(packs[s], 'seq', crossed(s))]
    all_to_all x1, waiting for transfers between devices: 0.01 us -> 2.37 us  [local(): lax.all_to_all(sent, 'seq', split_axis=0, concat_axis=0, tiled=True, axis...]
    ppermute x3, waiting for transfers between devices: 15.5 us -> 13.4 us  [local(): lax.ppermute(sums[s], 'seq', shifted(0, s))]
    all_to_all x1, starting transfers between devices: 5.38 us -> 7.37 us  [local(): lax.all_to_all(solved, 'seq', split_axis=0, concat_axis=0, tiled=True, ax...]
  transfers between devices with their start and end apart: 23 -> 23, of which waited for: 10 -> 7; matrix products, arithmetic and copies ran while one was open for 0% -> 0% of each run, Pallas kernels for 15% -> 17%
where the time goes in v2:
time: 150 us; the launch traced here: 148 us
  waiting for transfers between devices  56.8 us (38%)
  starting transfers between devices  52.5 us (35%)
  Pallas kernels  27.1 us (18%)
  local copies, waits for them, and re-layouts  9.08 us (6%)
  between operations  2.08 us (1%)
    pallas_call x12, Pallas kernels, call(): return lambda *args: made(*args, *after)  27.1 us
    ppermute x3, waiting for transfers between devices, local(): lax.ppermute(packs[s], 'seq', crossed(s))  24.8 us
    ppermute x3, waiting for transfers between devices, local(): lax.ppermute(done[s], 'seq', crossed(s))  13.6 us
    ppermute x3, waiting for transfers between devices, local(): lax.ppermute(sums[s], 'seq', shifted(0, s))  13.4 us
    ppermute x3, starting transfers between devices, local(): lax.ppermute(sums[s], 'seq', shifted(0, s))  13.1 us
    ppermute x3, starting transfers between devices, local(): lax.ppermute(caps, 'seq', shifted(0, -s))  10.1 us
    unnamed x20, local copies, waits for them, and re-layouts  9.07 us
    all_to_all x1, starting transfers between devices, local(): lax.all_to_all(solved, 'seq', split_axis=0, concat_axis=0, tiled=True, ax...  7.37 us
  transfers between devices with their start and end apart: 23, of which 7 were waited for; matrix products, arithmetic and copies ran while one was open for 0% of the time, Pallas kernels for 17%

profile of v2, /device:TPU:2, one launch (start us, length us, event | category | flops | bytes accessed | tf_op | source)
XLA Modules:
  0.0 147.8 jit_solution(16763578147334670920)
XLA Ops:
  1.4 6.3 %collective-permute-start = (bf16[2,5,1536]{2,1,0:T(8,128)(2,1)S(1)}, bf16[2,5,1536]{2,1,0:T(8,128)(2,1)S(1)}, u32[]{:S(2)}, u32[]{:S(2)}) collective-permute-start(bf16[2,5,1536]{2,1,0:T(8,128)(2,1)S(1)} %bitcast.7), channel_id=1, source_target_pairs={{0,12},{1,13},{2,14},{3,15},{4,0},{5,1},{6,2},{7,3},{8,4},{9,5},{1... | collective-permute-start | bytes 92168 | tf_op jit(solution)/shard_map/ppermute | solution.py:305
  8.7 2.8 %collective-permute-start.2 = (bf16[2,5,1536]{2,1,0:T(8,128)(2,1)S(1)}, bf16[2,5,1536]{2,1,0:T(8,128)(2,1)S(1)}, u32[]{:S(2)}, u32[]{:S(2)}) collective-permute-start(bf16[2,5,1536]{2,1,0:T(8,128)(2,1)S(1)} %bitcast.9), channel_id=1, source_target_pairs={{0,4},{1,5},{2,6},{3,7},{4,8},{5,9},{6,10},{7,11},{8,12},{9,13},{1... | collective-permute-start | bytes 92168 | tf_op jit(solution)/shard_map/ppermute | solution.py:305
  16.2 1.7 %frame_pack.1 = (bf16[704,384]{1,0:T(8,128)(2,1)S(1)}, bf16[704,384]{1,0:T(8,128)(2,1)}, bf16[704,384]{1,0:T(8,128)(2,1)}, bf16[704,384]{1,0:T(8,128)(2,1)}) custom-call(s32[4]{0:T(128)S(1)} %pad_add_fusion.refs_0_, bf16[3,128,1536]{2,1,0:T(8,128)(2,1)S(1)} %copy-done.4, bf16[128,1536]{1,0:T(8,128)(2,1)S(1)} %copy-done.2, bf16[128,1536]{1,0:T(8,128)(2,1)S(1)} %copy-done.7), custom_call_target="tpu_custom_call" | custom-call | bytes 1000 | tf_op jit(solution)/shard_map/frame_pack/pallas_call | solution.py:259
  21.0 1.3 temporal_pack.1
  22.3 6.7 %all-to-all-start = ((bf16[16,64,768]{2,1,0:T(8,128)(2,1)}), bf16[16,64,768]{2,1,0:T(8,128)(2,1)S(1)}, u32[]{:S(2)}, u32[]{:S(2)}) async-start(bf16[16,64,768]{2,1,0:T(8,128)(2,1)} %temporal_pack.1), calls=%async_computation | async-start | bytes 3145728 | tf_op jit(solution)/shard_map/all_to_all | solution.py:329
  29.0 13.8 %collective-permute-done.4.refs_2_.refs_3_.refs_7_ = bf16[704,384]{1,0:T(8,128)(2,1)S(1)} collective-permute-done((bf16[704,384]{1,0:T(8,128)(2,1)}, bf16[704,384]{1,0:T(8,128)(2,1)S(1)}, u32[]{:S(2)}, u32[]{:S(2)}) %collective-permute-start.4) | collective-permute-done | bytes 540704 | tf_op jit(solution)/shard_map/ppermute | solution.py:318
  42.9 10.9 %collective-permute-done.5.refs_3_.refs_4_.refs_8_ = bf16[704,384]{1,0:T(8,128)(2,1)} collective-permute-done((bf16[704,384]{1,0:T(8,128)(2,1)}, bf16[704,384]{1,0:T(8,128)(2,1)}, u32[]{:S(2)}, u32[]{:S(2)}) %collective-permute-start.5) | collective-permute-done | bytes 540704 | tf_op jit(solution)/shard_map/ppermute | solution.py:318
  54.6 3.1 %collective-permute-start.6 = (bf16[80,768]{1,0:T(8,128)(2,1)S(1)}, bf16[80,768]{1,0:T(8,128)(2,1)S(1)}, u32[]{:S(2)}, u32[]{:S(2)}) collective-permute-start(bf16[80,768]{1,0:T(8,128)(2,1)S(1)} %cap_join.1.refs_9_.refs_13_), channel_id=1, source_target_pairs={{0,48},{1,49},{2,50},{3,51},{4,52},{5,53},{6,54},{7,55},{8,56},{9,... | collective-permute-start | bytes 368648 | tf_op jit(solution)/shard_map/ppermute | solution.py:356
  59.3 6.4 %spatial_attention.1 = (bf16[640,384]{1,0:T(8,128)(2,1)S(1)}, bf16[640,384]{1,0:T(8,128)(2,1)S(1)}, bf16[640,384]{1,0:T(8,128)(2,1)}, bf16[640,384]{1,0:T(8,128)(2,1)}) custom-call(s32[4]{0:T(128)S(1)} %pad_add_fusion.refs_0_, bf16[704,384]{1,0:T(8,128)(2,1)S(1)} %get-tuple-element.42.refs_2_.refs_0_.refs_1_.refs_5_, ...), custom_call_target="tpu_custom_call" | custom-call | flops 99999997952 | bytes 4000000 | tf_op jit(solution)/shard_map/spatial_attention/pallas_call | solution.py:259
  65.7 1.7 %collective-permute-done.8.refs_12_.refs_16_ = bf16[80,768]{1,0:T(8,128)(2,1)S(1)} collective-permute-done((bf16[80,768]{1,0:T(8,128)(2,1)S(1)}, bf16[80,768]{1,0:T(8,128)(2,1)S(1)}, u32[]{:S(2)}, u32[]{:S(2)}) %collective-permute-start.8) | collective-permute-done | bytes 122912 | tf_op jit(solution)/shard_map/ppermute | solution.py:356
  67.4 5.2 %cross_attention.1 = (bf16[640,384]{1,0:T(8,128)(2,1)S(1)}, bf16[640,384]{1,0:T(8,128)(2,1)S(1)}, bf16[640,384]{1,0:T(8,128)(2,1)}, bf16[640,384]{1,0:T(8,128)(2...) custom-call(s32[4]{0:T(128)S(1)} %pad_add_fusion.refs_0_, ...), custom_call_target="tpu_custom_call", output_to_operand_aliasing={{0}: (17, {}), {1}: (18, {}), {2}: (19, {}), {3}: (20, {})} | custom-call | flops 1000000000 | bytes 3000000 | tf_op jit(solution)/shard_map/cross_attention/pallas_call | solution.py:259
  73.4 1.3 collective-permute-start.10
  76.5 2.5 %collective-permute-start.13 = (bf16[2,80,384]{2,1,0:T(8,128)(2,1)}, bf16[2,80,384]{2,1,0:T(8,128)(2,1)S(1)}, u32[]{:S(2)}, u32[]{:S(2)}) collective-permute-start(bf16[2,80,384]{2,1,0:T(8,128)(2,1)} %get-tuple-element.61), channel_id=1, source_target_pairs={{0,32},{1,33},{2,34},{3,35},{4,36},{5,37},{6,38},{7,39},{8,40},{9,... | collective-permute-start | bytes 368648 | tf_op jit(solution)/shard_map/ppermute | solution.py:391
  79.2 2.4 %all-to-all-done.refs_1_ = bf16[16,64,768]{2,1,0:T(8,128)(2,1)S(1)} async-done(((bf16[16,64,768]{2,1,0:T(8,128)(2,1)}), bf16[16,64,768]{2,1,0:T(8,128)(2,1)S(1)}, u32[]{:S(2)}, u32[]{:S(2)}) %all-to-all-start) | async-done | bytes 1572896 | tf_op jit(solution)/shard_map/all_to_all | solution.py:329
  81.5 5.0 %temporal_attention.1.refs_5_ = bf16[16,64,768]{2,1,0:T(8,128)(2,1)S(1)} custom-call(s32[4]{0:T(128)S(1)} %pad_add_fusion.refs_0_, bf16[16,64,768]{2,1,0:T(8,128)(2,1)S(1)} %all-to-all-done.refs_1_, bf16[640,384]{1,0:T(8,128)(2,1)S(1)} %collective-permute-done.9.refs_2_), custom_call_target="tpu_custom_call" | custom-call | flops 1000000 | bytes 10000 | tf_op jit(solution)/shard_map/temporal_attention/pallas_call | solution.py:259
  87.7 7.4 %all-to-all-start.1 = ((bf16[16,64,768]{2,1,0:T(8,128)(2,1)}), bf16[16,64,768]{2,1,0:T(8,128)(2,1)S(1)}, u32[]{:S(2)}, u32[]{:S(2)}) async-start(bf16[16,64,768]{2,1,0:T(8,128)(2,1)} %copy-done), calls=%async_computation.1 | async-start | bytes 3145728 | tf_op jit(solution)/shard_map/all_to_all | solution.py:388
  95.1 13.6 %collective-permute-done.11.refs_4_ = bf16[640,384]{1,0:T(8,128)(2,1)} collective-permute-done((bf16[640,384]{1,0:T(8,128)(2,1)}, bf16[640,384]{1,0:T(8,128)(2,1)}, u32[]{:S(2)}, u32[]{:S(2)}) %collective-permute-start.11) | collective-permute-done | bytes 491552 | tf_op jit(solution)/shard_map/ppermute | solution.py:375
  108.7 1.4 copy-done.1
  110.1 2.5 %frame_unpack.1 = (bf16[128,1536]{1,0:T(8,128)(2,1)S(1)}, bf16[3,128,1536]{2,1,0:T(8,128)(2,1)}, bf16[128,1536]{1,0:T(8,128)(2,1)}) custom-call(s32[4]{0:T(128)S(1)} %pad_add_fusion.refs_0_, bf16[640,384]{1,0:T(8,128)(2,1)S(1)} %copy-done.6, bf16[640,384]{1,0:T(8,128)(2,1)S(1)} %collective-permute-done.9.refs_2_, ...), custom_call_target="tpu_custom_call" | custom-call | flops 99999997952 | bytes 4000000 | tf_op jit(solution)/shard_map/frame_unpack/pallas_call | solution.py:259
  112.8 9.4 %collective-permute-start.15 = (bf16[2,32,384]{2,1,0:T(8,128)(2,1)S(1)}, bf16[2,32,384]{2,1,0:T(8,128)(2,1)S(1)}, u32[]{:S(2)}, u32[]{:S(2)}) collective-permute-start(bf16[2,32,384]{2,1,0:T(8,128)(2,1)S(1)} %get-tuple-element.64), channel_id=1, source_target_pairs={{0,4},{1,5},{2,6},{3,7},{4,8},{5,9},{6,10},{7,11},{8,12},{9,13},{1... | collective-permute-start | bytes 147464 | tf_op jit(solution)/shard_map/ppermute | solution.py:413
  122.2 3.7 %collective-permute-start.17 = (bf16[2,32,384]{2,1,0:T(8,128)(2,1)S(1)}, bf16[2,32,384]{2,1,0:T(8,128)(2,1)S(1)}, u32[]{:S(2)}, u32[]{:S(2)}) collective-permute-start(bf16[2,32,384]{2,1,0:T(8,128)(2,1)S(1)} %get-tuple-element.66), channel_id=1, source_target_pairs={{0,12},{1,13},{2,14},{3,15},{4,0},{5,1},{6,2},{7,3},{8,4},{9,5},{1... | collective-permute-start | bytes 147464 | tf_op jit(solution)/shard_map/ppermute | solution.py:413
  125.9 13.4 %collective-permute-done.15.refs_1_ = bf16[2,32,384]{2,1,0:T(8,128)(2,1)S(1)} collective-permute-done((bf16[2,32,384]{2,1,0:T(8,128)(2,1)S(1)}, bf16[2,32,384]{2,1,0:T(8,128)(2,1)S(1)}, u32[]{:S(2)}, u32[]{:S(2)}) %collective-permute-start.15) | collective-permute-done | bytes 49184 | tf_op jit(solution)/shard_map/ppermute | solution.py:413
  139.4 2.8 %collective-permute-start.19 = (f32[2,8,384]{2,1,0:T(8,128)S(1)}, f32[2,8,384]{2,1,0:T(8,128)S(1)}, u32[]{:S(2)}, u32[]{:S(2)}) collective-permute-start(f32[2,8,384]{2,1,0:T(8,128)S(1)} %get-tuple-element.69), channel_id=1, source_target_pairs={{0,2},{1,3},{2,0},{3,1},{4,6},{5,7},{6,4},{7,5},{8,10},{9,11},{10,... | collective-permute-start | bytes 73736 | tf_op jit(solution)/shard_map/ppermute | solution.py:423
  142.3 2.2 %temporal_unpack.1 = (bf16[128,1536]{1,0:T(8,128)(2,1)}, bf16[3,128,1536]{2,1,0:T(8,128)(2,1)}) custom-call(s32[4]{0:T(128)S(1)} %pad_add_fusion.refs_0_, bf16[16,64,768]{2,1,0:T(8,128)(2,1)S(1)} %all-to-all-done.1.refs_1_, bf16[128,1536]{1,0:T(8,128)(2,1)S(1)} %get-tuple-element.54.refs_2_.refs_4_), custom_call_target="tpu_custom_call" | custom-call | bytes 3600000 | tf_op jit(solution)/shard_map/temporal_unpack/pallas_call | solution.py:259
  (56 shorter events, 18.1 us)
Async XLA Ops:
  1.4 16.5 %collective-permute-start = (bf16[2,5,1536]{2,1,0:T(8,128)(2,1)S(1)}, bf16[2,5,1536]{2,1,0:T(8,128)(2,1)S(1)}, u32[]{:S(2)}, u32[]{:S(2)}) collective-permute-start(bf16[2,5,1536]{2,1,0:T(8,128)(2,1)S(1)} %bitcast.7), channel_id=1, source_target_pairs={{0,12},{1,13},{2,14},{3,15},{4,0},{5,1},{6,2},{7,3},{8,4},{9,5},{1... | collective-permute-start | bytes 92168 | tf_op jit(solution)/shard_map/ppermute | solution.py:305
  7.7 10.2 %collective-permute-start.1 = (bf16[2,5,1536]{2,1,0:T(8,128)(2,1)S(1)}, bf16[2,5,1536]{2,1,0:T(8,128)(2,1)S(1)}, u32[]{:S(2)}, u32[]{:S(2)}) collective-permute-start(bf16[2,5,1536]{2,1,0:T(8,128)(2,1)S(1)} %bitcast.8), channel_id=1, source_target_pairs={{0,8},{1,9},{2,10},{3,11},{4,12},{5,13},{6,14},{7,15},{8,0},{9,1},... | collective-permute-start | bytes 92168 | tf_op jit(solution)/shard_map/ppermute | solution.py:305
  8.7 9.2 %collective-permute-start.2 = (bf16[2,5,1536]{2,1,0:T(8,128)(2,1)S(1)}, bf16[2,5,1536]{2,1,0:T(8,128)(2,1)S(1)}, u32[]{:S(2)}, u32[]{:S(2)}) collective-permute-start(bf16[2,5,1536]{2,1,0:T(8,128)(2,1)S(1)} %bitcast.9), channel_id=1, source_target_pairs={{0,4},{1,5},{2,6},{3,7},{4,8},{5,9},{6,10},{7,11},{8,12},{9,13},{1... | collective-permute-start | bytes 92168 | tf_op jit(solution)/shard_map/ppermute | solution.py:305
  19.1 9.9 %collective-permute-start.3 = (bf16[704,384]{1,0:T(8,128)(2,1)}, bf16[704,384]{1,0:T(8,128)(2,1)S(1)}, u32[]{:S(2)}, u32[]{:S(2)}) collective-permute-start(bf16[704,384]{1,0:T(8,128)(2,1)} %get-tuple-element.43), channel_id=1, source_target_pairs={{0,1},{1,0},{2,3},{3,2},{4,5},{5,4},{6,7},{7,6},{8,9},{9,8},{10,11... | collective-permute-start | bytes 1622024 | tf_op jit(solution)/shard_map/ppermute | solution.py:318
  19.1 23.7 %collective-permute-start.4 = (bf16[704,384]{1,0:T(8,128)(2,1)}, bf16[704,384]{1,0:T(8,128)(2,1)S(1)}, u32[]{:S(2)}, u32[]{:S(2)}) collective-permute-start(bf16[704,384]{1,0:T(8,128)(2,1)} %get-tuple-element.44), channel_id=1, source_target_pairs={{0,2},{1,3},{2,0},{3,1},{4,6},{5,7},{6,4},{7,5},{8,10},{9,11},{10,... | collective-permute-start | bytes 1622024 | tf_op jit(solution)/shard_map/ppermute | solution.py:318
  20.2 33.6 %collective-permute-start.5 = (bf16[704,384]{1,0:T(8,128)(2,1)}, bf16[704,384]{1,0:T(8,128)(2,1)}, u32[]{:S(2)}, u32[]{:S(2)}) collective-permute-start(bf16[704,384]{1,0:T(8,128)(2,1)} %get-tuple-element.45), channel_id=1, source_target_pairs={{0,3},{1,2},{2,1},{3,0},{4,7},{5,6},{6,5},{7,4},{8,11},{9,10},{10,... | collective-permute-start | bytes 1622024 | tf_op jit(solution)/shard_map/ppermute | solution.py:318
  22.3 59.2 %all-to-all-start = ((bf16[16,64,768]{2,1,0:T(8,128)(2,1)}), bf16[16,64,768]{2,1,0:T(8,128)(2,1)S(1)}, u32[]{:S(2)}, u32[]{:S(2)}) async-start(bf16[16,64,768]{2,1,0:T(8,128)(2,1)} %temporal_pack.1), calls=%async_computation | async-start | bytes 3145728 | tf_op jit(solution)/shard_map/all_to_all | solution.py:329
  54.6 11.1 %collective-permute-start.6 = (bf16[80,768]{1,0:T(8,128)(2,1)S(1)}, bf16[80,768]{1,0:T(8,128)(2,1)S(1)}, u32[]{:S(2)}, u32[]{:S(2)}) collective-permute-start(bf16[80,768]{1,0:T(8,128)(2,1)S(1)} %cap_join.1.refs_9_.refs_13_), channel_id=1, source_target_pairs={{0,48},{1,49},{2,50},{3,51},{4,52},{5,53},{6,54},{7,55},{8,56},{9,... | collective-permute-start | bytes 368648 | tf_op jit(solution)/shard_map/ppermute | solution.py:356
  57.7 8.0 %collective-permute-start.7 = (bf16[80,768]{1,0:T(8,128)(2,1)S(1)}, bf16[80,768]{1,0:T(8,128)(2,1)S(1)}, u32[]{:S(2)}, u32[]{:S(2)}) collective-permute-start(bf16[80,768]{1,0:T(8,128)(2,1)S(1)} %cap_join.1.refs_9_.refs_13_), channel_id=1, source_target_pairs={{0,32},{1,33},{2,34},{3,35},{4,36},{5,37},{6,38},{7,39},{8,40},{9,... | collective-permute-start | bytes 368648 | tf_op jit(solution)/shard_map/ppermute | solution.py:356
  58.3 9.0 %collective-permute-start.8 = (bf16[80,768]{1,0:T(8,128)(2,1)S(1)}, bf16[80,768]{1,0:T(8,128)(2,1)S(1)}, u32[]{:S(2)}, u32[]{:S(2)}) collective-permute-start(bf16[80,768]{1,0:T(8,128)(2,1)S(1)} %cap_join.1.refs_9_.refs_13_), channel_id=1, source_target_pairs={{0,16},{1,17},{2,18},{3,19},{4,20},{5,21},{6,22},{7,23},{8,24},{9,... | collective-permute-start | bytes 368648 | tf_op jit(solution)/shard_map/ppermute | solution.py:356
  73.4 5.6 %collective-permute-start.9 = (bf16[640,384]{1,0:T(8,128)(2,1)S(1)}, bf16[640,384]{1,0:T(8,128)(2,1)S(1)}, u32[]{:S(2)}, u32[]{:S(2)}) collective-permute-start(bf16[640,384]{1,0:T(8,128)(2,1)S(1)} %get-tuple-element.50), channel_id=1, source_target_pairs={{0,1},{1,0},{2,3},{3,2},{4,5},{5,4},{6,7},{7,6},{8,9},{9,8},{10,11... | collective-permute-start | bytes 1474568 | tf_op jit(solution)/shard_map/ppermute | solution.py:375
  73.4 21.7 %collective-permute-start.10 = (bf16[640,384]{1,0:T(8,128)(2,1)}, bf16[640,384]{1,0:T(8,128)(2,1)}, u32[]{:S(2)}, u32[]{:S(2)}) collective-permute-start(bf16[640,384]{1,0:T(8,128)(2,1)} %get-tuple-element.52), channel_id=1, source_target_pairs={{0,2},{1,3},{2,0},{3,1},{4,6},{5,7},{6,4},{7,5},{8,10},{9,11},{10,... | collective-permute-start | bytes 1474568 | tf_op jit(solution)/shard_map/ppermute | solution.py:375
  74.7 34.0 %collective-permute-start.11 = (bf16[640,384]{1,0:T(8,128)(2,1)}, bf16[640,384]{1,0:T(8,128)(2,1)}, u32[]{:S(2)}, u32[]{:S(2)}) collective-permute-start(bf16[640,384]{1,0:T(8,128)(2,1)} %get-tuple-element.53), channel_id=1, source_target_pairs={{0,3},{1,2},{2,1},{3,0},{4,7},{5,6},{6,5},{7,4},{8,11},{9,10},{10,... | collective-permute-start | bytes 1474568 | tf_op jit(solution)/shard_map/ppermute | solution.py:375
  75.3 37.4 %collective-permute-start.12 = (bf16[2,80,384]{2,1,0:T(8,128)(2,1)}, bf16[2,80,384]{2,1,0:T(8,128)(2,1)S(1)}, u32[]{:S(2)}, u32[]{:S(2)}) collective-permute-start(bf16[2,80,384]{2,1,0:T(8,128)(2,1)} %get-tuple-element.60), channel_id=1, source_target_pairs={{0,16},{1,17},{2,18},{3,19},{4,20},{5,21},{6,22},{7,23},{8,24},{9,... | collective-permute-start | bytes 368648 | tf_op jit(solution)/shard_map/ppermute | solution.py:391
  76.5 36.1 %collective-permute-start.13 = (bf16[2,80,384]{2,1,0:T(8,128)(2,1)}, bf16[2,80,384]{2,1,0:T(8,128)(2,1)S(1)}, u32[]{:S(2)}, u32[]{:S(2)}) collective-permute-start(bf16[2,80,384]{2,1,0:T(8,128)(2,1)} %get-tuple-element.61), channel_id=1, source_target_pairs={{0,32},{1,33},{2,34},{3,35},{4,36},{5,37},{6,38},{7,39},{8,40},{9,... | collective-permute-start | bytes 368648 | tf_op jit(solution)/shard_map/ppermute | solution.py:391
  79.0 33.6 %collective-permute-start.14 = (bf16[2,80,384]{2,1,0:T(8,128)(2,1)}, bf16[2,80,384]{2,1,0:T(8,128)(2,1)S(1)}, u32[]{:S(2)}, u32[]{:S(2)}) collective-permute-start(bf16[2,80,384]{2,1,0:T(8,128)(2,1)} %get-tuple-element.62), channel_id=1, source_target_pairs={{0,48},{1,49},{2,50},{3,51},{4,52},{5,53},{6,54},{7,55},{8,56},{9,... | collective-permute-start | bytes 368648 | tf_op jit(solution)/shard_map/ppermute | solution.py:391
  87.7 21.0 %copy-start.6 = (bf16[640,384]{1,0:T(8,128)(2,1)S(1)}, bf16[640,384]{1,0:T(8,128)(2,1)}, u32[]{:S(2)}) copy-start(bf16[640,384]{1,0:T(8,128)(2,1)} %copy-done.5) | copy-start | bytes 1474564
  87.7 54.6 %all-to-all-start.1 = ((bf16[16,64,768]{2,1,0:T(8,128)(2,1)}), bf16[16,64,768]{2,1,0:T(8,128)(2,1)S(1)}, u32[]{:S(2)}, u32[]{:S(2)}) async-start(bf16[16,64,768]{2,1,0:T(8,128)(2,1)} %copy-done), calls=%async_computation.1 | async-start | bytes 3145728 | tf_op jit(solution)/shard_map/all_to_all | solution.py:388
  112.8 26.5 %collective-permute-start.15 = (bf16[2,32,384]{2,1,0:T(8,128)(2,1)S(1)}, bf16[2,32,384]{2,1,0:T(8,128)(2,1)S(1)}, u32[]{:S(2)}, u32[]{:S(2)}) collective-permute-start(bf16[2,32,384]{2,1,0:T(8,128)(2,1)S(1)} %get-tuple-element.64), channel_id=1, source_target_pairs={{0,4},{1,5},{2,6},{3,7},{4,8},{5,9},{6,10},{7,11},{8,12},{9,13},{1... | collective-permute-start | bytes 147464 | tf_op jit(solution)/shard_map/ppermute | solution.py:413
  122.2 17.1 %collective-permute-start.16 = (bf16[2,32,384]{2,1,0:T(8,128)(2,1)S(1)}, bf16[2,32,384]{2,1,0:T(8,128)(2,1)S(1)}, u32[]{:S(2)}, u32[]{:S(2)}) collective-permute-start(bf16[2,32,384]{2,1,0:T(8,128)(2,1)S(1)} %get-tuple-element.65), channel_id=1, source_target_pairs={{0,8},{1,9},{2,10},{3,11},{4,12},{5,13},{6,14},{7,15},{8,0},{9,1},... | collective-permute-start | bytes 147464 | tf_op jit(solution)/shard_map/ppermute | solution.py:413
  122.2 17.1 %collective-permute-start.17 = (bf16[2,32,384]{2,1,0:T(8,128)(2,1)S(1)}, bf16[2,32,384]{2,1,0:T(8,128)(2,1)S(1)}, u32[]{:S(2)}, u32[]{:S(2)}) collective-permute-start(bf16[2,32,384]{2,1,0:T(8,128)(2,1)S(1)} %get-tuple-element.66), channel_id=1, source_target_pairs={{0,12},{1,13},{2,14},{3,15},{4,0},{5,1},{6,2},{7,3},{8,4},{9,5},{1... | collective-permute-start | bytes 147464 | tf_op jit(solution)/shard_map/ppermute | solution.py:413
  139.3 5.2 %collective-permute-start.18 = (f32[2,8,384]{2,1,0:T(8,128)S(1)}, f32[2,8,384]{2,1,0:T(8,128)S(1)}, u32[]{:S(2)}, u32[]{:S(2)}) collective-permute-start(f32[2,8,384]{2,1,0:T(8,128)S(1)} %get-tuple-element.68), channel_id=1, source_target_pairs={{0,1},{1,0},{2,3},{3,2},{4,5},{5,4},{6,7},{7,6},{8,9},{9,8},{10,11... | collective-permute-start | bytes 73736 | tf_op jit(solution)/shard_map/ppermute | solution.py:423
  139.4 5.1 %collective-permute-start.19 = (f32[2,8,384]{2,1,0:T(8,128)S(1)}, f32[2,8,384]{2,1,0:T(8,128)S(1)}, u32[]{:S(2)}, u32[]{:S(2)}) collective-permute-start(f32[2,8,384]{2,1,0:T(8,128)S(1)} %get-tuple-element.69), channel_id=1, source_target_pairs={{0,2},{1,3},{2,0},{3,1},{4,6},{5,7},{6,4},{7,5},{8,10},{9,11},{10,... | collective-permute-start | bytes 73736 | tf_op jit(solution)/shard_map/ppermute | solution.py:423
  142.3 3.3 %collective-permute-start.20 = (f32[2,8,384]{2,1,0:T(8,128)S(1)}, f32[2,8,384]{2,1,0:T(8,128)S(1)}, u32[]{:S(2)}, u32[]{:S(2)}) collective-permute-start(f32[2,8,384]{2,1,0:T(8,128)S(1)} %get-tuple-element.70), channel_id=1, source_target_pairs={{0,3},{1,2},{2,1},{3,0},{4,7},{5,6},{6,5},{7,4},{8,11},{9,10},{10,... | collective-permute-start | bytes 73736 | tf_op jit(solution)/shard_map/ppermute | solution.py:423
  (8 other events, 10.8 us)

commit v3 on v2

--- a/solution.py
+++ b/solution.py
@@ -17,6 +17,7 @@
 FRAMES = 16
 CAP_ROWS = 320
 CAP_PAD = 32
+CAP_SUMS = 48
 MESSAGE = 5 * ROWS + 2 * CAP_PAD
 SCALE = HDIM**-0.5
 EXP2_SCALE = SCALE * 1.4426950408889634
@@ -125,17 +126,21 @@
 
 def cap_sum_y_kernel(p0, p1, p2, p3, o0, o1, o2, o3, rows, picked):
     rows[...] = sum(part[...].astype(F32) for part in (p0, p1, p2, p3))
+    picked[...] = jnp.zeros_like(picked)
     for z, out in enumerate((o0, o1, o2, o3)):
-        for s in range(4):
-            first = 20 * s + 5 * z
-            picked[:, 5 * s : 5 * (s + 1), :] = rows[:, first : first + 5, :]
+        for kind in range(2):
+            for s in range(4):
+                first, last = 20 * s + 5 * z, 20 * kind + 5 * s
+                picked[last : last + 5, :] = rows[kind, first : first + 5, :]
         out[...] = picked[...].astype(BF16)
 
 
 def cap_sum_z_kernel(p0, p1, p2, p3, o0, o1, o2, o3, rows):
     rows[...] = sum(part[...].astype(F32) for part in (p0, p1, p2, p3))
     for s, out in enumerate((o0, o1, o2, o3)):
-        out[...] = rows[:, 5 * s : 5 * s + 8, :]
+        for kind in range(2):
+            first = 20 * kind + 5 * s
+            out[kind, :, :] = rows[first : first + 8, :]
 
 
 def cap_place_kernel(scal, p0, p1, p2, p3, out):
@@ -201,7 +206,8 @@
             grads[i, :, lanes] = part[(i + 2) * ROWS : (i + 3) * ROWS, :]
 
 
-def temporal_unpack_kernel(scal, back, both, mixed, grads):
+def temporal_unpack_kernel(scal, back, both, mixed, grads, token):
+    token[...] = jnp.zeros_like(token)
     first = (scal[1] * 4 + scal[0]) * ROWS + pl.program_id(0) * PIXELS * (back.shape[0] // 2)
     row = lax.broadcasted_iota(jnp.int32, (PIXELS, HALF), 0)
     for group in range(back.shape[0] // 2):
@@ -402,13 +408,13 @@
 
     sums = call(
         cap_sum_y_kernel,
-        [low(2, CAP_PAD, QUARTER)] * 4,
+        [low(CAP_SUMS, QUARTER)] * 4,
         [spec()] * 4,
         [spec()] * 4,
         moved=700_000,
         name="cap_sum_y",
         after=(both,),
-        scratch=[pltpu.VMEM((2, 80, QUARTER), F32), pltpu.VMEM((2, CAP_PAD, QUARTER), F32)],
+        scratch=[pltpu.VMEM((2, 80, QUARTER), F32), pltpu.VMEM((CAP_SUMS, QUARTER), F32)],
     )(*sums)
     sums = [sums[0]] + [lax.ppermute(sums[s], "seq", shifted(0, s)) for s in (1, 2, 3)]
     sums = call(
@@ -418,13 +424,13 @@
         [spec()] * 4,
         moved=300_000,
         name="cap_sum_z",
-        scratch=[pltpu.VMEM((2, CAP_PAD, QUARTER), F32)],
+        scratch=[pltpu.VMEM((CAP_SUMS, QUARTER), F32)],
     )(*sums)
     sums = [sums[0]] + [lax.ppermute(sums[s], "seq", crossed(s)) for s in (1, 2, 3)]
     steps = 4
-    mixed, temporal_grads = call(
+    mixed, temporal_grads, token = call(
         temporal_unpack_kernel,
-        [low(ROWS, WIDTH), low(3, ROWS, WIDTH)],
+        [low(ROWS, WIDTH), low(3, ROWS, WIDTH), full(8, HDIM)],
         [
             SMEM,
             spec((16 // steps, 4 * PIXELS, HALF), lambda i: (i, 0, 0)),
@@ -433,6 +439,7 @@
         [
             spec((ROWS // steps, WIDTH), lambda i: (i, 0)),
             spec((3, ROWS // steps, WIDTH), lambda i: (0, i, 0)),
+            spec((8, HDIM), lambda i: (0, 0)),
         ],
         grid=(steps,),
         moved=3_600_000,
@@ -446,7 +453,7 @@
         spec(),
         moved=200_000,
         name="cap_place",
-        after=(mixed,),
+        after=(token,),
     )(scal, *sums)
     caption_grads = jnp.swapaxes(sums[:, :5], 0, 1)
     return (mixed, spatial_grads, temporal_grads, cross_query_grad, caption_grads)

time: 150 us -> 147 us (0.980)
    unnamed x20 -> x18, local copies, waits for them, and re-layouts: 9.07 us -> 8.08 us
where the time goes in v3:
time: 147 us; the launch traced here: 146 us
  waiting for transfers between devices  56 us (38%)
  starting transfers between devices  52.3 us (36%)
  Pallas kernels  27.1 us (18%)
  local copies, waits for them, and re-layouts  8.09 us (6%)
  between operations  2.08 us (1%)
    pallas_call x12, Pallas kernels, call(): return lambda *args: made(*args, *after)  27.1 us
    ppermute x3, waiting for transfers between devices, local(): lax.ppermute(packs[s], 'seq', crossed(s))  24.8 us
    ppermute x3, waiting for transfers between devices, local(): lax.ppermute(done[s], 'seq', crossed(s))  13.6 us
    ppermute x3, starting transfers between devices, local(): lax.ppermute(sums[s], 'seq', shifted(0, s))  13.1 us
    ppermute x3, waiting for transfers between devices, local(): lax.ppermute(sums[s], 'seq', shifted(0, s))  12.7 us
    ppermute x3, starting transfers between devices, local(): lax.ppermute(caps, 'seq', shifted(0, -s))  10.1 us
    unnamed x18, local copies, waits for them, and re-layouts  8.08 us
    all_to_all x1, starting transfers between devices, local(): lax.all_to_all(solved, 'seq', split_axis=0, concat_axis=0, tiled=True, ax...  7.42 us
  transfers between devices with their start and end apart: 23, of which 7 were waited for; matrix products, arithmetic and copies ran while one was open for 0% of the time, Pallas kernels for 17%

profile of v3, /device:TPU:2, one launch (start us, length us, event | category | flops | bytes accessed | tf_op | source)
XLA Modules:
  0.0 145.7 jit_solution(6269914820600230970)
XLA Ops:
  1.4 6.3 %collective-permute-start = (bf16[2,5,1536]{2,1,0:T(8,128)(2,1)S(1)}, bf16[2,5,1536]{2,1,0:T(8,128)(2,1)S(1)}, u32[]{:S(2)}, u32[]{:S(2)}) collective-permute-start(bf16[2,5,1536]{2,1,0:T(8,128)(2,1)S(1)} %bitcast.7), channel_id=1, source_target_pairs={{0,12},{1,13},{2,14},{3,15},{4,0},{5,1},{6,2},{7,3},{8,4},{9,5},{1... | collective-permute-start | bytes 92168 | tf_op jit(solution)/shard_map/ppermute | solution.py:311
  8.7 2.8 %collective-permute-start.2 = (bf16[2,5,1536]{2,1,0:T(8,128)(2,1)S(1)}, bf16[2,5,1536]{2,1,0:T(8,128)(2,1)S(1)}, u32[]{:S(2)}, u32[]{:S(2)}) collective-permute-start(bf16[2,5,1536]{2,1,0:T(8,128)(2,1)S(1)} %bitcast.9), channel_id=1, source_target_pairs={{0,4},{1,5},{2,6},{3,7},{4,8},{5,9},{6,10},{7,11},{8,12},{9,13},{1... | collective-permute-start | bytes 92168 | tf_op jit(solution)/shard_map/ppermute | solution.py:311
  16.2 1.7 %frame_pack.1 = (bf16[704,384]{1,0:T(8,128)(2,1)S(1)}, bf16[704,384]{1,0:T(8,128)(2,1)}, bf16[704,384]{1,0:T(8,128)(2,1)}, bf16[704,384]{1,0:T(8,128)(2,1)}) custom-call(s32[4]{0:T(128)S(1)} %pad_add_fusion.refs_0_, bf16[3,128,1536]{2,1,0:T(8,128)(2,1)S(1)} %copy-done.4, bf16[128,1536]{1,0:T(8,128)(2,1)S(1)} %copy-done.2, bf16[128,1536]{1,0:T(8,128)(2,1)S(1)} %copy-done.7), custom_call_target="tpu_custom_call" | custom-call | bytes 1000 | tf_op jit(solution)/shard_map/frame_pack/pallas_call | solution.py:265
  21.0 1.3 temporal_pack.1
  22.3 6.7 %all-to-all-start = ((bf16[16,64,768]{2,1,0:T(8,128)(2,1)}), bf16[16,64,768]{2,1,0:T(8,128)(2,1)S(1)}, u32[]{:S(2)}, u32[]{:S(2)}) async-start(bf16[16,64,768]{2,1,0:T(8,128)(2,1)} %temporal_pack.1), calls=%async_computation | async-start | bytes 3145728 | tf_op jit(solution)/shard_map/all_to_all | solution.py:335
  29.0 13.8 %collective-permute-done.4.refs_2_.refs_3_.refs_7_ = bf16[704,384]{1,0:T(8,128)(2,1)S(1)} collective-permute-done((bf16[704,384]{1,0:T(8,128)(2,1)}, bf16[704,384]{1,0:T(8,128)(2,1)S(1)}, u32[]{:S(2)}, u32[]{:S(2)}) %collective-permute-start.4) | collective-permute-done | bytes 540704 | tf_op jit(solution)/shard_map/ppermute | solution.py:324
  42.9 10.9 %collective-permute-done.5.refs_3_.refs_4_.refs_8_ = bf16[704,384]{1,0:T(8,128)(2,1)} collective-permute-done((bf16[704,384]{1,0:T(8,128)(2,1)}, bf16[704,384]{1,0:T(8,128)(2,1)}, u32[]{:S(2)}, u32[]{:S(2)}) %collective-permute-start.5) | collective-permute-done | bytes 540704 | tf_op jit(solution)/shard_map/ppermute | solution.py:324
  54.6 3.1 %collective-permute-start.6 = (bf16[80,768]{1,0:T(8,128)(2,1)S(1)}, bf16[80,768]{1,0:T(8,128)(2,1)S(1)}, u32[]{:S(2)}, u32[]{:S(2)}) collective-permute-start(bf16[80,768]{1,0:T(8,128)(2,1)S(1)} %cap_join.1.refs_9_.refs_13_), channel_id=1, source_target_pairs={{0,48},{1,49},{2,50},{3,51},{4,52},{5,53},{6,54},{7,55},{8,56},{9,... | collective-permute-start | bytes 368648 | tf_op jit(solution)/shard_map/ppermute | solution.py:362
  59.3 6.3 %spatial_attention.1 = (bf16[640,384]{1,0:T(8,128)(2,1)S(1)}, bf16[640,384]{1,0:T(8,128)(2,1)S(1)}, bf16[640,384]{1,0:T(8,128)(2,1)}, bf16[640,384]{1,0:T(8,128)(2,1)}) custom-call(s32[4]{0:T(128)S(1)} %pad_add_fusion.refs_0_, bf16[704,384]{1,0:T(8,128)(2,1)S(1)} %get-tuple-element.43.refs_2_.refs_0_.refs_1_.refs_5_, ...), custom_call_target="tpu_custom_call" | custom-call | flops 99999997952 | bytes 4000000 | tf_op jit(solution)/shard_map/spatial_attention/pallas_call | solution.py:265
  65.7 1.7 %collective-permute-done.8.refs_12_.refs_16_ = bf16[80,768]{1,0:T(8,128)(2,1)S(1)} collective-permute-done((bf16[80,768]{1,0:T(8,128)(2,1)S(1)}, bf16[80,768]{1,0:T(8,128)(2,1)S(1)}, u32[]{:S(2)}, u32[]{:S(2)}) %collective-permute-start.8) | collective-permute-done | bytes 122912 | tf_op jit(solution)/shard_map/ppermute | solution.py:362
  67.4 5.3 %cross_attention.1 = (bf16[640,384]{1,0:T(8,128)(2,1)S(1)}, bf16[640,384]{1,0:T(8,128)(2,1)S(1)}, bf16[640,384]{1,0:T(8,128)(2,1)}, bf16[640,384]{1,0:T(8,128)(2...) custom-call(s32[4]{0:T(128)S(1)} %pad_add_fusion.refs_0_, ...), custom_call_target="tpu_custom_call", output_to_operand_aliasing={{0}: (17, {}), {1}: (18, {}), {2}: (19, {}), {3}: (20, {})} | custom-call | flops 1000000000 | bytes 3000000 | tf_op jit(solution)/shard_map/cross_attention/pallas_call | solution.py:265
  73.5 1.3 collective-permute-start.10
  76.5 2.5 %collective-permute-start.13 = (bf16[2,80,384]{2,1,0:T(8,128)(2,1)}, bf16[2,80,384]{2,1,0:T(8,128)(2,1)S(1)}, u32[]{:S(2)}, u32[]{:S(2)}) collective-permute-start(bf16[2,80,384]{2,1,0:T(8,128)(2,1)} %get-tuple-element.62), channel_id=1, source_target_pairs={{0,32},{1,33},{2,34},{3,35},{4,36},{5,37},{6,38},{7,39},{8,40},{9,... | collective-permute-start | bytes 368648 | tf_op jit(solution)/shard_map/ppermute | solution.py:397
  79.2 2.3 %all-to-all-done.refs_1_ = bf16[16,64,768]{2,1,0:T(8,128)(2,1)S(1)} async-done(((bf16[16,64,768]{2,1,0:T(8,128)(2,1)}), bf16[16,64,768]{2,1,0:T(8,128)(2,1)S(1)}, u32[]{:S(2)}, u32[]{:S(2)}) %all-to-all-start) | async-done | bytes 1572896 | tf_op jit(solution)/shard_map/all_to_all | solution.py:335
  81.5 5.0 %temporal_attention.1.refs_5_ = bf16[16,64,768]{2,1,0:T(8,128)(2,1)S(1)} custom-call(s32[4]{0:T(128)S(1)} %pad_add_fusion.refs_0_, bf16[16,64,768]{2,1,0:T(8,128)(2,1)S(1)} %all-to-all-done.refs_1_, bf16[640,384]{1,0:T(8,128)(2,1)S(1)} %collective-permute-done.9.refs_2_), custom_call_target="tpu_custom_call" | custom-call | flops 1000000 | bytes 10000 | tf_op jit(solution)/shard_map/temporal_attention/pallas_call | solution.py:265
  87.7 7.4 %all-to-all-start.1 = ((bf16[16,64,768]{2,1,0:T(8,128)(2,1)}), bf16[16,64,768]{2,1,0:T(8,128)(2,1)S(1)}, u32[]{:S(2)}, u32[]{:S(2)}) async-start(bf16[16,64,768]{2,1,0:T(8,128)(2,1)} %copy-done), calls=%async_computation.1 | async-start | bytes 3145728 | tf_op jit(solution)/shard_map/all_to_all | solution.py:394
  95.2 13.6 %collective-permute-done.11.refs_4_ = bf16[640,384]{1,0:T(8,128)(2,1)} collective-permute-done((bf16[640,384]{1,0:T(8,128)(2,1)}, bf16[640,384]{1,0:T(8,128)(2,1)}, u32[]{:S(2)}, u32[]{:S(2)}) %collective-permute-start.11) | collective-permute-done | bytes 491552 | tf_op jit(solution)/shard_map/ppermute | solution.py:381
  108.7 1.4 copy-done.1
  110.2 2.5 %frame_unpack.1 = (bf16[128,1536]{1,0:T(8,128)(2,1)S(1)}, bf16[3,128,1536]{2,1,0:T(8,128)(2,1)}, bf16[128,1536]{1,0:T(8,128)(2,1)}) custom-call(s32[4]{0:T(128)S(1)} %pad_add_fusion.refs_0_, bf16[640,384]{1,0:T(8,128)(2,1)S(1)} %copy-done.6, bf16[640,384]{1,0:T(8,128)(2,1)S(1)} %collective-permute-done.9.refs_2_, ...), custom_call_target="tpu_custom_call" | custom-call | flops 99999997952 | bytes 4000000 | tf_op jit(solution)/shard_map/frame_unpack/pallas_call | solution.py:265
  112.8 9.4 %collective-permute-start.15 = (bf16[48,384]{1,0:T(8,128)(2,1)S(1)}, bf16[48,384]{1,0:T(8,128)(2,1)S(1)}, u32[]{:S(2)}, u32[]{:S(2)}) collective-permute-start(bf16[48,384]{1,0:T(8,128)(2,1)S(1)} %get-tuple-element.65), channel_id=1, source_target_pairs={{0,4},{1,5},{2,6},{3,7},{4,8},{5,9},{6,10},{7,11},{8,12},{9,13},{1... | collective-permute-start | bytes 110600 | tf_op jit(solution)/shard_map/ppermute | solution.py:419
  122.2 3.7 %collective-permute-start.17 = (bf16[48,384]{1,0:T(8,128)(2,1)S(1)}, bf16[48,384]{1,0:T(8,128)(2,1)S(1)}, u32[]{:S(2)}, u32[]{:S(2)}) collective-permute-start(bf16[48,384]{1,0:T(8,128)(2,1)S(1)} %get-tuple-element.67), channel_id=1, source_target_pairs={{0,12},{1,13},{2,14},{3,15},{4,0},{5,1},{6,2},{7,3},{8,4},{9,5},{1... | collective-permute-start | bytes 110600 | tf_op jit(solution)/shard_map/ppermute | solution.py:419
  125.9 12.7 %collective-permute-done.15.refs_1_ = bf16[48,384]{1,0:T(8,128)(2,1)S(1)} collective-permute-done((bf16[48,384]{1,0:T(8,128)(2,1)S(1)}, bf16[48,384]{1,0:T(8,128)(2,1)S(1)}, u32[]{:S(2)}, u32[]{:S(2)}) %collective-permute-start.15) | collective-permute-done | bytes 36896 | tf_op jit(solution)/shard_map/ppermute | solution.py:419
  138.7 2.5 %collective-permute-start.19 = (f32[2,8,384]{2,1,0:T(8,128)S(1)}, f32[2,8,384]{2,1,0:T(8,128)S(1)}, u32[]{:S(2)}, u32[]{:S(2)}) collective-permute-start(f32[2,8,384]{2,1,0:T(8,128)S(1)} %get-tuple-element.70), channel_id=1, source_target_pairs={{0,2},{1,3},{2,0},{3,1},{4,6},{5,7},{6,4},{7,5},{8,10},{9,11},{10,... | collective-permute-start | bytes 73736 | tf_op jit(solution)/shard_map/ppermute | solution.py:429
  141.3 2.2 %temporal_unpack.1 = (bf16[128,1536]{1,0:T(8,128)(2,1)}, bf16[3,128,1536]{2,1,0:T(8,128)(2,1)}, f32[8,128]{1,0:T(8,128)S(1)}) custom-call(s32[4]{0:T(128)S(1)} %pad_add_fusion.refs_0_, bf16[16,64,768]{2,1,0:T(8,128)(2,1)S(1)} %all-to-all-done.1.refs_1_, bf16[128,1536]{1,0:T(8,128)(2,1)S(1)} %get-tuple-element.55.refs_2_.refs_4_), custom_call_target="tpu_custom_call" | custom-call | bytes 3600000 | tf_op jit(solution)/shard_map/temporal_unpack/pallas_call | solution.py:265
  (54 shorter events, 17.1 us)
Async XLA Ops:
  1.4 16.5 %collective-permute-start = (bf16[2,5,1536]{2,1,0:T(8,128)(2,1)S(1)}, bf16[2,5,1536]{2,1,0:T(8,128)(2,1)S(1)}, u32[]{:S(2)}, u32[]{:S(2)}) collective-permute-start(bf16[2,5,1536]{2,1,0:T(8,128)(2,1)S(1)} %bitcast.7), channel_id=1, source_target_pairs={{0,12},{1,13},{2,14},{3,15},{4,0},{5,1},{6,2},{7,3},{8,4},{9,5},{1... | collective-permute-start | bytes 92168 | tf_op jit(solution)/shard_map/ppermute | solution.py:311
  7.7 10.2 %collective-permute-start.1 = (bf16[2,5,1536]{2,1,0:T(8,128)(2,1)S(1)}, bf16[2,5,1536]{2,1,0:T(8,128)(2,1)S(1)}, u32[]{:S(2)}, u32[]{:S(2)}) collective-permute-start(bf16[2,5,1536]{2,1,0:T(8,128)(2,1)S(1)} %bitcast.8), channel_id=1, source_target_pairs={{0,8},{1,9},{2,10},{3,11},{4,12},{5,13},{6,14},{7,15},{8,0},{9,1},... | collective-permute-start | bytes 92168 | tf_op jit(solution)/shard_map/ppermute | solution.py:311
  8.7 9.2 %collective-permute-start.2 = (bf16[2,5,1536]{2,1,0:T(8,128)(2,1)S(1)}, bf16[2,5,1536]{2,1,0:T(8,128)(2,1)S(1)}, u32[]{:S(2)}, u32[]{:S(2)}) collective-permute-start(bf16[2,5,1536]{2,1,0:T(8,128)(2,1)S(1)} %bitcast.9), channel_id=1, source_target_pairs={{0,4},{1,5},{2,6},{3,7},{4,8},{5,9},{6,10},{7,11},{8,12},{9,13},{1... | collective-permute-start | bytes 92168 | tf_op jit(solution)/shard_map/ppermute | solution.py:311
  19.1 9.9 %collective-permute-start.3 = (bf16[704,384]{1,0:T(8,128)(2,1)}, bf16[704,384]{1,0:T(8,128)(2,1)S(1)}, u32[]{:S(2)}, u32[]{:S(2)}) collective-permute-start(bf16[704,384]{1,0:T(8,128)(2,1)} %get-tuple-element.44), channel_id=1, source_target_pairs={{0,1},{1,0},{2,3},{3,2},{4,5},{5,4},{6,7},{7,6},{8,9},{9,8},{10,11... | collective-permute-start | bytes 1622024 | tf_op jit(solution)/shard_map/ppermute | solution.py:324
  19.1 23.7 %collective-permute-start.4 = (bf16[704,384]{1,0:T(8,128)(2,1)}, bf16[704,384]{1,0:T(8,128)(2,1)S(1)}, u32[]{:S(2)}, u32[]{:S(2)}) collective-permute-start(bf16[704,384]{1,0:T(8,128)(2,1)} %get-tuple-element.45), channel_id=1, source_target_pairs={{0,2},{1,3},{2,0},{3,1},{4,6},{5,7},{6,4},{7,5},{8,10},{9,11},{10,... | collective-permute-start | bytes 1622024 | tf_op jit(solution)/shard_map/ppermute | solution.py:324
  20.2 33.6 %collective-permute-start.5 = (bf16[704,384]{1,0:T(8,128)(2,1)}, bf16[704,384]{1,0:T(8,128)(2,1)}, u32[]{:S(2)}, u32[]{:S(2)}) collective-permute-start(bf16[704,384]{1,0:T(8,128)(2,1)} %get-tuple-element.46), channel_id=1, source_target_pairs={{0,3},{1,2},{2,1},{3,0},{4,7},{5,6},{6,5},{7,4},{8,11},{9,10},{10,... | collective-permute-start | bytes 1622024 | tf_op jit(solution)/shard_map/ppermute | solution.py:324
  22.3 59.2 %all-to-all-start = ((bf16[16,64,768]{2,1,0:T(8,128)(2,1)}), bf16[16,64,768]{2,1,0:T(8,128)(2,1)S(1)}, u32[]{:S(2)}, u32[]{:S(2)}) async-start(bf16[16,64,768]{2,1,0:T(8,128)(2,1)} %temporal_pack.1), calls=%async_computation | async-start | bytes 3145728 | tf_op jit(solution)/shard_map/all_to_all | solution.py:335
  54.6 11.0 %collective-permute-start.6 = (bf16[80,768]{1,0:T(8,128)(2,1)S(1)}, bf16[80,768]{1,0:T(8,128)(2,1)S(1)}, u32[]{:S(2)}, u32[]{:S(2)}) collective-permute-start(bf16[80,768]{1,0:T(8,128)(2,1)S(1)} %cap_join.1.refs_9_.refs_13_), channel_id=1, source_target_pairs={{0,48},{1,49},{2,50},{3,51},{4,52},{5,53},{6,54},{7,55},{8,56},{9,... | collective-permute-start | bytes 368648 | tf_op jit(solution)/shard_map/ppermute | solution.py:362
  57.7 8.0 %collective-permute-start.7 = (bf16[80,768]{1,0:T(8,128)(2,1)S(1)}, bf16[80,768]{1,0:T(8,128)(2,1)S(1)}, u32[]{:S(2)}, u32[]{:S(2)}) collective-permute-start(bf16[80,768]{1,0:T(8,128)(2,1)S(1)} %cap_join.1.refs_9_.refs_13_), channel_id=1, source_target_pairs={{0,32},{1,33},{2,34},{3,35},{4,36},{5,37},{6,38},{7,39},{8,40},{9,... | collective-permute-start | bytes 368648 | tf_op jit(solution)/shard_map/ppermute | solution.py:362
  58.3 9.0 %collective-permute-start.8 = (bf16[80,768]{1,0:T(8,128)(2,1)S(1)}, bf16[80,768]{1,0:T(8,128)(2,1)S(1)}, u32[]{:S(2)}, u32[]{:S(2)}) collective-permute-start(bf16[80,768]{1,0:T(8,128)(2,1)S(1)} %cap_join.1.refs_9_.refs_13_), channel_id=1, source_target_pairs={{0,16},{1,17},{2,18},{3,19},{4,20},{5,21},{6,22},{7,23},{8,24},{9,... | collective-permute-start | bytes 368648 | tf_op jit(solution)/shard_map/ppermute | solution.py:362
  73.4 5.6 %collective-permute-start.9 = (bf16[640,384]{1,0:T(8,128)(2,1)S(1)}, bf16[640,384]{1,0:T(8,128)(2,1)S(1)}, u32[]{:S(2)}, u32[]{:S(2)}) collective-permute-start(bf16[640,384]{1,0:T(8,128)(2,1)S(1)} %get-tuple-element.51), channel_id=1, source_target_pairs={{0,1},{1,0},{2,3},{3,2},{4,5},{5,4},{6,7},{7,6},{8,9},{9,8},{10,11... | collective-permute-start | bytes 1474568 | tf_op jit(solution)/shard_map/ppermute | solution.py:381
  73.5 21.7 %collective-permute-start.10 = (bf16[640,384]{1,0:T(8,128)(2,1)}, bf16[640,384]{1,0:T(8,128)(2,1)}, u32[]{:S(2)}, u32[]{:S(2)}) collective-permute-start(bf16[640,384]{1,0:T(8,128)(2,1)} %get-tuple-element.53), channel_id=1, source_target_pairs={{0,2},{1,3},{2,0},{3,1},{4,6},{5,7},{6,4},{7,5},{8,10},{9,11},{10,... | collective-permute-start | bytes 1474568 | tf_op jit(solution)/shard_map/ppermute | solution.py:381
  74.8 34.0 %collective-permute-start.11 = (bf16[640,384]{1,0:T(8,128)(2,1)}, bf16[640,384]{1,0:T(8,128)(2,1)}, u32[]{:S(2)}, u32[]{:S(2)}) collective-permute-start(bf16[640,384]{1,0:T(8,128)(2,1)} %get-tuple-element.54), channel_id=1, source_target_pairs={{0,3},{1,2},{2,1},{3,0},{4,7},{5,6},{6,5},{7,4},{8,11},{9,10},{10,... | collective-permute-start | bytes 1474568 | tf_op jit(solution)/shard_map/ppermute | solution.py:381
  75.3 37.3 %collective-permute-start.12 = (bf16[2,80,384]{2,1,0:T(8,128)(2,1)}, bf16[2,80,384]{2,1,0:T(8,128)(2,1)S(1)}, u32[]{:S(2)}, u32[]{:S(2)}) collective-permute-start(bf16[2,80,384]{2,1,0:T(8,128)(2,1)} %get-tuple-element.61), channel_id=1, source_target_pairs={{0,16},{1,17},{2,18},{3,19},{4,20},{5,21},{6,22},{7,23},{8,24},{9,... | collective-permute-start | bytes 368648 | tf_op jit(solution)/shard_map/ppermute | solution.py:397
  76.5 36.1 %collective-permute-start.13 = (bf16[2,80,384]{2,1,0:T(8,128)(2,1)}, bf16[2,80,384]{2,1,0:T(8,128)(2,1)S(1)}, u32[]{:S(2)}, u32[]{:S(2)}) collective-permute-start(bf16[2,80,384]{2,1,0:T(8,128)(2,1)} %get-tuple-element.62), channel_id=1, source_target_pairs={{0,32},{1,33},{2,34},{3,35},{4,36},{5,37},{6,38},{7,39},{8,40},{9,... | collective-permute-start | bytes 368648 | tf_op jit(solution)/shard_map/ppermute | solution.py:397
  79.1 33.6 %collective-permute-start.14 = (bf16[2,80,384]{2,1,0:T(8,128)(2,1)}, bf16[2,80,384]{2,1,0:T(8,128)(2,1)S(1)}, u32[]{:S(2)}, u32[]{:S(2)}) collective-permute-start(bf16[2,80,384]{2,1,0:T(8,128)(2,1)} %get-tuple-element.63), channel_id=1, source_target_pairs={{0,48},{1,49},{2,50},{3,51},{4,52},{5,53},{6,54},{7,55},{8,56},{9,... | collective-permute-start | bytes 368648 | tf_op jit(solution)/shard_map/ppermute | solution.py:397
  87.7 21.0 %copy-start.6 = (bf16[640,384]{1,0:T(8,128)(2,1)S(1)}, bf16[640,384]{1,0:T(8,128)(2,1)}, u32[]{:S(2)}) copy-start(bf16[640,384]{1,0:T(8,128)(2,1)} %copy-done.5) | copy-start | bytes 1474564
  87.7 53.5 %all-to-all-start.1 = ((bf16[16,64,768]{2,1,0:T(8,128)(2,1)}), bf16[16,64,768]{2,1,0:T(8,128)(2,1)S(1)}, u32[]{:S(2)}, u32[]{:S(2)}) async-start(bf16[16,64,768]{2,1,0:T(8,128)(2,1)} %copy-done), calls=%async_computation.1 | async-start | bytes 3145728 | tf_op jit(solution)/shard_map/all_to_all | solution.py:394
  112.8 25.7 %collective-permute-start.15 = (bf16[48,384]{1,0:T(8,128)(2,1)S(1)}, bf16[48,384]{1,0:T(8,128)(2,1)S(1)}, u32[]{:S(2)}, u32[]{:S(2)}) collective-permute-start(bf16[48,384]{1,0:T(8,128)(2,1)S(1)} %get-tuple-element.65), channel_id=1, source_target_pairs={{0,4},{1,5},{2,6},{3,7},{4,8},{5,9},{6,10},{7,11},{8,12},{9,13},{1... | collective-permute-start | bytes 110600 | tf_op jit(solution)/shard_map/ppermute | solution.py:419
  122.2 16.3 %collective-permute-start.16 = (bf16[48,384]{1,0:T(8,128)(2,1)S(1)}, bf16[48,384]{1,0:T(8,128)(2,1)S(1)}, u32[]{:S(2)}, u32[]{:S(2)}) collective-permute-start(bf16[48,384]{1,0:T(8,128)(2,1)S(1)} %get-tuple-element.66), channel_id=1, source_target_pairs={{0,8},{1,9},{2,10},{3,11},{4,12},{5,13},{6,14},{7,15},{8,0},{9,1},... | collective-permute-start | bytes 110600 | tf_op jit(solution)/shard_map/ppermute | solution.py:419
  122.2 16.3 %collective-permute-start.17 = (bf16[48,384]{1,0:T(8,128)(2,1)S(1)}, bf16[48,384]{1,0:T(8,128)(2,1)S(1)}, u32[]{:S(2)}, u32[]{:S(2)}) collective-permute-start(bf16[48,384]{1,0:T(8,128)(2,1)S(1)} %get-tuple-element.67), channel_id=1, source_target_pairs={{0,12},{1,13},{2,14},{3,15},{4,0},{5,1},{6,2},{7,3},{8,4},{9,5},{1... | collective-permute-start | bytes 110600 | tf_op jit(solution)/shard_map/ppermute | solution.py:419
  138.6 4.9 %collective-permute-start.18 = (f32[2,8,384]{2,1,0:T(8,128)S(1)}, f32[2,8,384]{2,1,0:T(8,128)S(1)}, u32[]{:S(2)}, u32[]{:S(2)}) collective-permute-start(f32[2,8,384]{2,1,0:T(8,128)S(1)} %get-tuple-element.69), channel_id=1, source_target_pairs={{0,1},{1,0},{2,3},{3,2},{4,5},{5,4},{6,7},{7,6},{8,9},{9,8},{10,11... | collective-permute-start | bytes 73736 | tf_op jit(solution)/shard_map/ppermute | solution.py:429
  138.7 4.8 %collective-permute-start.19 = (f32[2,8,384]{2,1,0:T(8,128)S(1)}, f32[2,8,384]{2,1,0:T(8,128)S(1)}, u32[]{:S(2)}, u32[]{:S(2)}) collective-permute-start(f32[2,8,384]{2,1,0:T(8,128)S(1)} %get-tuple-element.70), channel_id=1, source_target_pairs={{0,2},{1,3},{2,0},{3,1},{4,6},{5,7},{6,4},{7,5},{8,10},{9,11},{10,... | collective-permute-start | bytes 73736 | tf_op jit(solution)/shard_map/ppermute | solution.py:429
  141.2 3.3 %collective-permute-start.20 = (f32[2,8,384]{2,1,0:T(8,128)S(1)}, f32[2,8,384]{2,1,0:T(8,128)S(1)}, u32[]{:S(2)}, u32[]{:S(2)}) collective-permute-start(f32[2,8,384]{2,1,0:T(8,128)S(1)} %get-tuple-element.71), channel_id=1, source_target_pairs={{0,3},{1,2},{2,1},{3,0},{4,7},{5,6},{6,5},{7,4},{8,11},{9,10},{10,... | collective-permute-start | bytes 73736 | tf_op jit(solution)/shard_map/ppermute | solution.py:429
  (7 other events, 9.8 us)

commit v4 on v3

--- a/solution.py
+++ b/solution.py
@@ -427,7 +427,7 @@
         scratch=[pltpu.VMEM((CAP_SUMS, QUARTER), F32)],
     )(*sums)
     sums = [sums[0]] + [lax.ppermute(sums[s], "seq", crossed(s)) for s in (1, 2, 3)]
-    steps = 4
+    steps = 2
     mixed, temporal_grads, token = call(
         temporal_unpack_kernel,
         [low(ROWS, WIDTH), low(3, ROWS, WIDTH), full(8, HDIM)],

time: 147 us -> 147 us (level)
  no operation moved by 1% of the time
where the time goes in v4:
time: 147 us; the launch traced here: 146 us
  waiting for transfers between devices  56.5 us (38%)
  starting transfers between devices  52.3 us (36%)
  Pallas kernels  26.6 us (18%)
  local copies, waits for them, and re-layouts  8.09 us (6%)
  between operations  2.08 us (1%)
    pallas_call x12, Pallas kernels, call(): return lambda *args: made(*args, *after)  26.6 us
    ppermute x3, waiting for transfers between devices, local(): lax.ppermute(packs[s], 'seq', crossed(s))  24.8 us
    ppermute x3, waiting for transfers between devices, local(): lax.ppermute(done[s], 'seq', crossed(s))  13.6 us
    ppermute x3, starting transfers between devices, local(): lax.ppermute(sums[s], 'seq', shifted(0, s))  13.1 us
    ppermute x3, waiting for transfers between devices, local(): lax.ppermute(sums[s], 'seq', shifted(0, s))  12.7 us
    ppermute x3, starting transfers between devices, local(): lax.ppermute(caps, 'seq', shifted(0, -s))  10.1 us
    unnamed x18, local copies, waits for them, and re-layouts  8.08 us
    all_to_all x1, starting transfers between devices, local(): lax.all_to_all(solved, 'seq', split_axis=0, concat_axis=0, tiled=True, ax...  7.42 us
  transfers between devices with their start and end apart: 23, of which 7 were waited for; matrix products, arithmetic and copies ran while one was open for 0% of the time, Pallas kernels for 17%

profile of v4, /device:TPU:2, one launch (start us, length us, event | category | flops | bytes accessed | tf_op | source)
XLA Modules:
  0.0 145.7 jit_solution(16681313419890823508)
XLA Ops:
  1.4 6.3 %collective-permute-start = (bf16[2,5,1536]{2,1,0:T(8,128)(2,1)S(1)}, bf16[2,5,1536]{2,1,0:T(8,128)(2,1)S(1)}, u32[]{:S(2)}, u32[]{:S(2)}) collective-permute-start(bf16[2,5,1536]{2,1,0:T(8,128)(2,1)S(1)} %bitcast.7), channel_id=1, source_target_pairs={{0,12},{1,13},{2,14},{3,15},{4,0},{5,1},{6,2},{7,3},{8,4},{9,5},{1... | collective-permute-start | bytes 92168 | tf_op jit(solution)/shard_map/ppermute | solution.py:311
  8.7 2.8 %collective-permute-start.2 = (bf16[2,5,1536]{2,1,0:T(8,128)(2,1)S(1)}, bf16[2,5,1536]{2,1,0:T(8,128)(2,1)S(1)}, u32[]{:S(2)}, u32[]{:S(2)}) collective-permute-start(bf16[2,5,1536]{2,1,0:T(8,128)(2,1)S(1)} %bitcast.9), channel_id=1, source_target_pairs={{0,4},{1,5},{2,6},{3,7},{4,8},{5,9},{6,10},{7,11},{8,12},{9,13},{1... | collective-permute-start | bytes 92168 | tf_op jit(solution)/shard_map/ppermute | solution.py:311
  16.2 1.7 %frame_pack.1 = (bf16[704,384]{1,0:T(8,128)(2,1)S(1)}, bf16[704,384]{1,0:T(8,128)(2,1)}, bf16[704,384]{1,0:T(8,128)(2,1)}, bf16[704,384]{1,0:T(8,128)(2,1)}) custom-call(s32[4]{0:T(128)S(1)} %pad_add_fusion.refs_0_, bf16[3,128,1536]{2,1,0:T(8,128)(2,1)S(1)} %copy-done.4, bf16[128,1536]{1,0:T(8,128)(2,1)S(1)} %copy-done.2, bf16[128,1536]{1,0:T(8,128)(2,1)S(1)} %copy-done.7), custom_call_target="tpu_custom_call" | custom-call | bytes 1000 | tf_op jit(solution)/shard_map/frame_pack/pallas_call | solution.py:265
  22.3 6.7 %all-to-all-start = ((bf16[16,64,768]{2,1,0:T(8,128)(2,1)}), bf16[16,64,768]{2,1,0:T(8,128)(2,1)S(1)}, u32[]{:S(2)}, u32[]{:S(2)}) async-start(bf16[16,64,768]{2,1,0:T(8,128)(2,1)} %temporal_pack.1), calls=%async_computation | async-start | bytes 3145728 | tf_op jit(solution)/shard_map/all_to_all | solution.py:335
  29.0 13.8 %collective-permute-done.4.refs_2_.refs_3_.refs_7_ = bf16[704,384]{1,0:T(8,128)(2,1)S(1)} collective-permute-done((bf16[704,384]{1,0:T(8,128)(2,1)}, bf16[704,384]{1,0:T(8,128)(2,1)S(1)}, u32[]{:S(2)}, u32[]{:S(2)}) %collective-permute-start.4) | collective-permute-done | bytes 540704 | tf_op jit(solution)/shard_map/ppermute | solution.py:324
  42.9 10.9 %collective-permute-done.5.refs_3_.refs_4_.refs_8_ = bf16[704,384]{1,0:T(8,128)(2,1)} collective-permute-done((bf16[704,384]{1,0:T(8,128)(2,1)}, bf16[704,384]{1,0:T(8,128)(2,1)}, u32[]{:S(2)}, u32[]{:S(2)}) %collective-permute-start.5) | collective-permute-done | bytes 540704 | tf_op jit(solution)/shard_map/ppermute | solution.py:324
  54.6 3.1 %collective-permute-start.6 = (bf16[80,768]{1,0:T(8,128)(2,1)S(1)}, bf16[80,768]{1,0:T(8,128)(2,1)S(1)}, u32[]{:S(2)}, u32[]{:S(2)}) collective-permute-start(bf16[80,768]{1,0:T(8,128)(2,1)S(1)} %cap_join.1.refs_9_.refs_13_), channel_id=1, source_target_pairs={{0,48},{1,49},{2,50},{3,51},{4,52},{5,53},{6,54},{7,55},{8,56},{9,... | collective-permute-start | bytes 368648 | tf_op jit(solution)/shard_map/ppermute | solution.py:362
  59.3 6.3 %spatial_attention.1 = (bf16[640,384]{1,0:T(8,128)(2,1)S(1)}, bf16[640,384]{1,0:T(8,128)(2,1)S(1)}, bf16[640,384]{1,0:T(8,128)(2,1)}, bf16[640,384]{1,0:T(8,128)(2,1)}) custom-call(s32[4]{0:T(128)S(1)} %pad_add_fusion.refs_0_, bf16[704,384]{1,0:T(8,128)(2,1)S(1)} %get-tuple-element.43.refs_2_.refs_0_.refs_1_.refs_5_, ...), custom_call_target="tpu_custom_call" | custom-call | flops 99999997952 | bytes 4000000 | tf_op jit(solution)/shard_map/spatial_attention/pallas_call | solution.py:265
  65.7 1.7 %collective-permute-done.8.refs_12_.refs_16_ = bf16[80,768]{1,0:T(8,128)(2,1)S(1)} collective-permute-done((bf16[80,768]{1,0:T(8,128)(2,1)S(1)}, bf16[80,768]{1,0:T(8,128)(2,1)S(1)}, u32[]{:S(2)}, u32[]{:S(2)}) %collective-permute-start.8) | collective-permute-done | bytes 122912 | tf_op jit(solution)/shard_map/ppermute | solution.py:362
  67.4 5.3 %cross_attention.1 = (bf16[640,384]{1,0:T(8,128)(2,1)S(1)}, bf16[640,384]{1,0:T(8,128)(2,1)S(1)}, bf16[640,384]{1,0:T(8,128)(2,1)}, bf16[640,384]{1,0:T(8,128)(2...) custom-call(s32[4]{0:T(128)S(1)} %pad_add_fusion.refs_0_, ...), custom_call_target="tpu_custom_call", output_to_operand_aliasing={{0}: (17, {}), {1}: (18, {}), {2}: (19, {}), {3}: (20, {})} | custom-call | flops 1000000000 | bytes 3000000 | tf_op jit(solution)/shard_map/cross_attention/pallas_call | solution.py:265
  73.5 1.3 collective-permute-start.10
  76.5 2.5 %collective-permute-start.13 = (bf16[2,80,384]{2,1,0:T(8,128)(2,1)}, bf16[2,80,384]{2,1,0:T(8,128)(2,1)S(1)}, u32[]{:S(2)}, u32[]{:S(2)}) collective-permute-start(bf16[2,80,384]{2,1,0:T(8,128)(2,1)} %get-tuple-element.62), channel_id=1, source_target_pairs={{0,32},{1,33},{2,34},{3,35},{4,36},{5,37},{6,38},{7,39},{8,40},{9,... | collective-permute-start | bytes 368648 | tf_op jit(solution)/shard_map/ppermute | solution.py:397
  79.2 2.3 %all-to-all-done.refs_1_ = bf16[16,64,768]{2,1,0:T(8,128)(2,1)S(1)} async-done(((bf16[16,64,768]{2,1,0:T(8,128)(2,1)}), bf16[16,64,768]{2,1,0:T(8,128)(2,1)S(1)}, u32[]{:S(2)}, u32[]{:S(2)}) %all-to-all-start) | async-done | bytes 1572896 | tf_op jit(solution)/shard_map/all_to_all | solution.py:335
  81.5 5.0 %temporal_attention.1.refs_5_ = bf16[16,64,768]{2,1,0:T(8,128)(2,1)S(1)} custom-call(s32[4]{0:T(128)S(1)} %pad_add_fusion.refs_0_, bf16[16,64,768]{2,1,0:T(8,128)(2,1)S(1)} %all-to-all-done.refs_1_, bf16[640,384]{1,0:T(8,128)(2,1)S(1)} %collective-permute-done.9.refs_2_), custom_call_target="tpu_custom_call" | custom-call | flops 1000000 | bytes 10000 | tf_op jit(solution)/shard_map/temporal_attention/pallas_call | solution.py:265
  87.7 7.4 %all-to-all-start.1 = ((bf16[16,64,768]{2,1,0:T(8,128)(2,1)}), bf16[16,64,768]{2,1,0:T(8,128)(2,1)S(1)}, u32[]{:S(2)}, u32[]{:S(2)}) async-start(bf16[16,64,768]{2,1,0:T(8,128)(2,1)} %copy-done), calls=%async_computation.1 | async-start | bytes 3145728 | tf_op jit(solution)/shard_map/all_to_all | solution.py:394
  95.2 13.6 %collective-permute-done.11.refs_4_ = bf16[640,384]{1,0:T(8,128)(2,1)} collective-permute-done((bf16[640,384]{1,0:T(8,128)(2,1)}, bf16[640,384]{1,0:T(8,128)(2,1)}, u32[]{:S(2)}, u32[]{:S(2)}) %collective-permute-start.11) | collective-permute-done | bytes 491552 | tf_op jit(solution)/shard_map/ppermute | solution.py:381
  108.7 1.4 copy-done.1
  110.2 2.5 %frame_unpack.1 = (bf16[128,1536]{1,0:T(8,128)(2,1)S(1)}, bf16[3,128,1536]{2,1,0:T(8,128)(2,1)}, bf16[128,1536]{1,0:T(8,128)(2,1)}) custom-call(s32[4]{0:T(128)S(1)} %pad_add_fusion.refs_0_, bf16[640,384]{1,0:T(8,128)(2,1)S(1)} %copy-done.6, bf16[640,384]{1,0:T(8,128)(2,1)S(1)} %collective-permute-done.9.refs_2_, ...), custom_call_target="tpu_custom_call" | custom-call | flops 99999997952 | bytes 4000000 | tf_op jit(solution)/shard_map/frame_unpack/pallas_call | solution.py:265
  112.8 9.4 %collective-permute-start.15 = (bf16[48,384]{1,0:T(8,128)(2,1)S(1)}, bf16[48,384]{1,0:T(8,128)(2,1)S(1)}, u32[]{:S(2)}, u32[]{:S(2)}) collective-permute-start(bf16[48,384]{1,0:T(8,128)(2,1)S(1)} %get-tuple-element.65), channel_id=1, source_target_pairs={{0,4},{1,5},{2,6},{3,7},{4,8},{5,9},{6,10},{7,11},{8,12},{9,13},{1... | collective-permute-start | bytes 110600 | tf_op jit(solution)/shard_map/ppermute | solution.py:419
  122.2 3.7 %collective-permute-start.17 = (bf16[48,384]{1,0:T(8,128)(2,1)S(1)}, bf16[48,384]{1,0:T(8,128)(2,1)S(1)}, u32[]{:S(2)}, u32[]{:S(2)}) collective-permute-start(bf16[48,384]{1,0:T(8,128)(2,1)S(1)} %get-tuple-element.67), channel_id=1, source_target_pairs={{0,12},{1,13},{2,14},{3,15},{4,0},{5,1},{6,2},{7,3},{8,4},{9,5},{1... | collective-permute-start | bytes 110600 | tf_op jit(solution)/shard_map/ppermute | solution.py:419
  125.9 12.7 %collective-permute-done.15.refs_1_ = bf16[48,384]{1,0:T(8,128)(2,1)S(1)} collective-permute-done((bf16[48,384]{1,0:T(8,128)(2,1)S(1)}, bf16[48,384]{1,0:T(8,128)(2,1)S(1)}, u32[]{:S(2)}, u32[]{:S(2)}) %collective-permute-start.15) | collective-permute-done | bytes 36896 | tf_op jit(solution)/shard_map/ppermute | solution.py:419
  138.7 2.5 %collective-permute-start.19 = (f32[2,8,384]{2,1,0:T(8,128)S(1)}, f32[2,8,384]{2,1,0:T(8,128)S(1)}, u32[]{:S(2)}, u32[]{:S(2)}) collective-permute-start(f32[2,8,384]{2,1,0:T(8,128)S(1)} %get-tuple-element.70), channel_id=1, source_target_pairs={{0,2},{1,3},{2,0},{3,1},{4,6},{5,7},{6,4},{7,5},{8,10},{9,11},{10,... | collective-permute-start | bytes 73736 | tf_op jit(solution)/shard_map/ppermute | solution.py:429
  141.3 1.8 %temporal_unpack.1 = (bf16[128,1536]{1,0:T(8,128)(2,1)}, bf16[3,128,1536]{2,1,0:T(8,128)(2,1)}, f32[8,128]{1,0:T(8,128)S(1)}) custom-call(s32[4]{0:T(128)S(1)} %pad_add_fusion.refs_0_, bf16[16,64,768]{2,1,0:T(8,128)(2,1)S(1)} %all-to-all-done.1.refs_1_, bf16[128,1536]{1,0:T(8,128)(2,1)S(1)} %get-tuple-element.55.refs_2_.refs_4_), custom_call_target="tpu_custom_call" | custom-call | bytes 3600000 | tf_op jit(solution)/shard_map/temporal_unpack/pallas_call | solution.py:265
  143.0 1.4 collective-permute-done.20.refs_4_
  (54 shorter events, 17.4 us)
Async XLA Ops:
  1.4 16.5 %collective-permute-start = (bf16[2,5,1536]{2,1,0:T(8,128)(2,1)S(1)}, bf16[2,5,1536]{2,1,0:T(8,128)(2,1)S(1)}, u32[]{:S(2)}, u32[]{:S(2)}) collective-permute-start(bf16[2,5,1536]{2,1,0:T(8,128)(2,1)S(1)} %bitcast.7), channel_id=1, source_target_pairs={{0,12},{1,13},{2,14},{3,15},{4,0},{5,1},{6,2},{7,3},{8,4},{9,5},{1... | collective-permute-start | bytes 92168 | tf_op jit(solution)/shard_map/ppermute | solution.py:311
  7.7 10.2 %collective-permute-start.1 = (bf16[2,5,1536]{2,1,0:T(8,128)(2,1)S(1)}, bf16[2,5,1536]{2,1,0:T(8,128)(2,1)S(1)}, u32[]{:S(2)}, u32[]{:S(2)}) collective-permute-start(bf16[2,5,1536]{2,1,0:T(8,128)(2,1)S(1)} %bitcast.8), channel_id=1, source_target_pairs={{0,8},{1,9},{2,10},{3,11},{4,12},{5,13},{6,14},{7,15},{8,0},{9,1},... | collective-permute-start | bytes 92168 | tf_op jit(solution)/shard_map/ppermute | solution.py:311
  8.7 9.2 %collective-permute-start.2 = (bf16[2,5,1536]{2,1,0:T(8,128)(2,1)S(1)}, bf16[2,5,1536]{2,1,0:T(8,128)(2,1)S(1)}, u32[]{:S(2)}, u32[]{:S(2)}) collective-permute-start(bf16[2,5,1536]{2,1,0:T(8,128)(2,1)S(1)} %bitcast.9), channel_id=1, source_target_pairs={{0,4},{1,5},{2,6},{3,7},{4,8},{5,9},{6,10},{7,11},{8,12},{9,13},{1... | collective-permute-start | bytes 92168 | tf_op jit(solution)/shard_map/ppermute | solution.py:311
  19.1 9.9 %collective-permute-start.3 = (bf16[704,384]{1,0:T(8,128)(2,1)}, bf16[704,384]{1,0:T(8,128)(2,1)S(1)}, u32[]{:S(2)}, u32[]{:S(2)}) collective-permute-start(bf16[704,384]{1,0:T(8,128)(2,1)} %get-tuple-element.44), channel_id=1, source_target_pairs={{0,1},{1,0},{2,3},{3,2},{4,5},{5,4},{6,7},{7,6},{8,9},{9,8},{10,11... | collective-permute-start | bytes 1622024 | tf_op jit(solution)/shard_map/ppermute | solution.py:324
  19.1 23.7 %collective-permute-start.4 = (bf16[704,384]{1,0:T(8,128)(2,1)}, bf16[704,384]{1,0:T(8,128)(2,1)S(1)}, u32[]{:S(2)}, u32[]{:S(2)}) collective-permute-start(bf16[704,384]{1,0:T(8,128)(2,1)} %get-tuple-element.45), channel_id=1, source_target_pairs={{0,2},{1,3},{2,0},{3,1},{4,6},{5,7},{6,4},{7,5},{8,10},{9,11},{10,... | collective-permute-start | bytes 1622024 | tf_op jit(solution)/shard_map/ppermute | solution.py:324
  20.2 33.6 %collective-permute-start.5 = (bf16[704,384]{1,0:T(8,128)(2,1)}, bf16[704,384]{1,0:T(8,128)(2,1)}, u32[]{:S(2)}, u32[]{:S(2)}) collective-permute-start(bf16[704,384]{1,0:T(8,128)(2,1)} %get-tuple-element.46), channel_id=1, source_target_pairs={{0,3},{1,2},{2,1},{3,0},{4,7},{5,6},{6,5},{7,4},{8,11},{9,10},{10,... | collective-permute-start | bytes 1622024 | tf_op jit(solution)/shard_map/ppermute | solution.py:324
  22.3 59.2 %all-to-all-start = ((bf16[16,64,768]{2,1,0:T(8,128)(2,1)}), bf16[16,64,768]{2,1,0:T(8,128)(2,1)S(1)}, u32[]{:S(2)}, u32[]{:S(2)}) async-start(bf16[16,64,768]{2,1,0:T(8,128)(2,1)} %temporal_pack.1), calls=%async_computation | async-start | bytes 3145728 | tf_op jit(solution)/shard_map/all_to_all | solution.py:335
  54.6 11.0 %collective-permute-start.6 = (bf16[80,768]{1,0:T(8,128)(2,1)S(1)}, bf16[80,768]{1,0:T(8,128)(2,1)S(1)}, u32[]{:S(2)}, u32[]{:S(2)}) collective-permute-start(bf16[80,768]{1,0:T(8,128)(2,1)S(1)} %cap_join.1.refs_9_.refs_13_), channel_id=1, source_target_pairs={{0,48},{1,49},{2,50},{3,51},{4,52},{5,53},{6,54},{7,55},{8,56},{9,... | collective-permute-start | bytes 368648 | tf_op jit(solution)/shard_map/ppermute | solution.py:362
  57.7 8.0 %collective-permute-start.7 = (bf16[80,768]{1,0:T(8,128)(2,1)S(1)}, bf16[80,768]{1,0:T(8,128)(2,1)S(1)}, u32[]{:S(2)}, u32[]{:S(2)}) collective-permute-start(bf16[80,768]{1,0:T(8,128)(2,1)S(1)} %cap_join.1.refs_9_.refs_13_), channel_id=1, source_target_pairs={{0,32},{1,33},{2,34},{3,35},{4,36},{5,37},{6,38},{7,39},{8,40},{9,... | collective-permute-start | bytes 368648 | tf_op jit(solution)/shard_map/ppermute | solution.py:362
  58.3 9.0 %collective-permute-start.8 = (bf16[80,768]{1,0:T(8,128)(2,1)S(1)}, bf16[80,768]{1,0:T(8,128)(2,1)S(1)}, u32[]{:S(2)}, u32[]{:S(2)}) collective-permute-start(bf16[80,768]{1,0:T(8,128)(2,1)S(1)} %cap_join.1.refs_9_.refs_13_), channel_id=1, source_target_pairs={{0,16},{1,17},{2,18},{3,19},{4,20},{5,21},{6,22},{7,23},{8,24},{9,... | collective-permute-start | bytes 368648 | tf_op jit(solution)/shard_map/ppermute | solution.py:362
  73.4 5.6 %collective-permute-start.9 = (bf16[640,384]{1,0:T(8,128)(2,1)S(1)}, bf16[640,384]{1,0:T(8,128)(2,1)S(1)}, u32[]{:S(2)}, u32[]{:S(2)}) collective-permute-start(bf16[640,384]{1,0:T(8,128)(2,1)S(1)} %get-tuple-element.51), channel_id=1, source_target_pairs={{0,1},{1,0},{2,3},{3,2},{4,5},{5,4},{6,7},{7,6},{8,9},{9,8},{10,11... | collective-permute-start | bytes 1474568 | tf_op jit(solution)/shard_map/ppermute | solution.py:381
  73.5 21.7 %collective-permute-start.10 = (bf16[640,384]{1,0:T(8,128)(2,1)}, bf16[640,384]{1,0:T(8,128)(2,1)}, u32[]{:S(2)}, u32[]{:S(2)}) collective-permute-start(bf16[640,384]{1,0:T(8,128)(2,1)} %get-tuple-element.53), channel_id=1, source_target_pairs={{0,2},{1,3},{2,0},{3,1},{4,6},{5,7},{6,4},{7,5},{8,10},{9,11},{10,... | collective-permute-start | bytes 1474568 | tf_op jit(solution)/shard_map/ppermute | solution.py:381
  74.8 34.0 %collective-permute-start.11 = (bf16[640,384]{1,0:T(8,128)(2,1)}, bf16[640,384]{1,0:T(8,128)(2,1)}, u32[]{:S(2)}, u32[]{:S(2)}) collective-permute-start(bf16[640,384]{1,0:T(8,128)(2,1)} %get-tuple-element.54), channel_id=1, source_target_pairs={{0,3},{1,2},{2,1},{3,0},{4,7},{5,6},{6,5},{7,4},{8,11},{9,10},{10,... | collective-permute-start | bytes 1474568 | tf_op jit(solution)/shard_map/ppermute | solution.py:381
  75.3 37.3 %collective-permute-start.12 = (bf16[2,80,384]{2,1,0:T(8,128)(2,1)}, bf16[2,80,384]{2,1,0:T(8,128)(2,1)S(1)}, u32[]{:S(2)}, u32[]{:S(2)}) collective-permute-start(bf16[2,80,384]{2,1,0:T(8,128)(2,1)} %get-tuple-element.61), channel_id=1, source_target_pairs={{0,16},{1,17},{2,18},{3,19},{4,20},{5,21},{6,22},{7,23},{8,24},{9,... | collective-permute-start | bytes 368648 | tf_op jit(solution)/shard_map/ppermute | solution.py:397
  76.5 36.1 %collective-permute-start.13 = (bf16[2,80,384]{2,1,0:T(8,128)(2,1)}, bf16[2,80,384]{2,1,0:T(8,128)(2,1)S(1)}, u32[]{:S(2)}, u32[]{:S(2)}) collective-permute-start(bf16[2,80,384]{2,1,0:T(8,128)(2,1)} %get-tuple-element.62), channel_id=1, source_target_pairs={{0,32},{1,33},{2,34},{3,35},{4,36},{5,37},{6,38},{7,39},{8,40},{9,... | collective-permute-start | bytes 368648 | tf_op jit(solution)/shard_map/ppermute | solution.py:397
  79.1 33.6 %collective-permute-start.14 = (bf16[2,80,384]{2,1,0:T(8,128)(2,1)}, bf16[2,80,384]{2,1,0:T(8,128)(2,1)S(1)}, u32[]{:S(2)}, u32[]{:S(2)}) collective-permute-start(bf16[2,80,384]{2,1,0:T(8,128)(2,1)} %get-tuple-element.63), channel_id=1, source_target_pairs={{0,48},{1,49},{2,50},{3,51},{4,52},{5,53},{6,54},{7,55},{8,56},{9,... | collective-permute-start | bytes 368648 | tf_op jit(solution)/shard_map/ppermute | solution.py:397
  87.7 21.0 %copy-start.6 = (bf16[640,384]{1,0:T(8,128)(2,1)S(1)}, bf16[640,384]{1,0:T(8,128)(2,1)}, u32[]{:S(2)}) copy-start(bf16[640,384]{1,0:T(8,128)(2,1)} %copy-done.5) | copy-start | bytes 1474564
  87.7 53.5 %all-to-all-start.1 = ((bf16[16,64,768]{2,1,0:T(8,128)(2,1)}), bf16[16,64,768]{2,1,0:T(8,128)(2,1)S(1)}, u32[]{:S(2)}, u32[]{:S(2)}) async-start(bf16[16,64,768]{2,1,0:T(8,128)(2,1)} %copy-done), calls=%async_computation.1 | async-start | bytes 3145728 | tf_op jit(solution)/shard_map/all_to_all | solution.py:394
  112.8 25.7 %collective-permute-start.15 = (bf16[48,384]{1,0:T(8,128)(2,1)S(1)}, bf16[48,384]{1,0:T(8,128)(2,1)S(1)}, u32[]{:S(2)}, u32[]{:S(2)}) collective-permute-start(bf16[48,384]{1,0:T(8,128)(2,1)S(1)} %get-tuple-element.65), channel_id=1, source_target_pairs={{0,4},{1,5},{2,6},{3,7},{4,8},{5,9},{6,10},{7,11},{8,12},{9,13},{1... | collective-permute-start | bytes 110600 | tf_op jit(solution)/shard_map/ppermute | solution.py:419
  122.2 16.3 %collective-permute-start.16 = (bf16[48,384]{1,0:T(8,128)(2,1)S(1)}, bf16[48,384]{1,0:T(8,128)(2,1)S(1)}, u32[]{:S(2)}, u32[]{:S(2)}) collective-permute-start(bf16[48,384]{1,0:T(8,128)(2,1)S(1)} %get-tuple-element.66), channel_id=1, source_target_pairs={{0,8},{1,9},{2,10},{3,11},{4,12},{5,13},{6,14},{7,15},{8,0},{9,1},... | collective-permute-start | bytes 110600 | tf_op jit(solution)/shard_map/ppermute | solution.py:419
  122.2 16.3 %collective-permute-start.17 = (bf16[48,384]{1,0:T(8,128)(2,1)S(1)}, bf16[48,384]{1,0:T(8,128)(2,1)S(1)}, u32[]{:S(2)}, u32[]{:S(2)}) collective-permute-start(bf16[48,384]{1,0:T(8,128)(2,1)S(1)} %get-tuple-element.67), channel_id=1, source_target_pairs={{0,12},{1,13},{2,14},{3,15},{4,0},{5,1},{6,2},{7,3},{8,4},{9,5},{1... | collective-permute-start | bytes 110600 | tf_op jit(solution)/shard_map/ppermute | solution.py:419
  138.6 4.4 %collective-permute-start.18 = (f32[2,8,384]{2,1,0:T(8,128)S(1)}, f32[2,8,384]{2,1,0:T(8,128)S(1)}, u32[]{:S(2)}, u32[]{:S(2)}) collective-permute-start(f32[2,8,384]{2,1,0:T(8,128)S(1)} %get-tuple-element.69), channel_id=1, source_target_pairs={{0,1},{1,0},{2,3},{3,2},{4,5},{5,4},{6,7},{7,6},{8,9},{9,8},{10,11... | collective-permute-start | bytes 73736 | tf_op jit(solution)/shard_map/ppermute | solution.py:429
  138.7 4.3 %collective-permute-start.19 = (f32[2,8,384]{2,1,0:T(8,128)S(1)}, f32[2,8,384]{2,1,0:T(8,128)S(1)}, u32[]{:S(2)}, u32[]{:S(2)}) collective-permute-start(f32[2,8,384]{2,1,0:T(8,128)S(1)} %get-tuple-element.70), channel_id=1, source_target_pairs={{0,2},{1,3},{2,0},{3,1},{4,6},{5,7},{6,4},{7,5},{8,10},{9,11},{10,... | collective-permute-start | bytes 73736 | tf_op jit(solution)/shard_map/ppermute | solution.py:429
  141.2 3.3 %collective-permute-start.20 = (f32[2,8,384]{2,1,0:T(8,128)S(1)}, f32[2,8,384]{2,1,0:T(8,128)S(1)}, u32[]{:S(2)}, u32[]{:S(2)}) collective-permute-start(f32[2,8,384]{2,1,0:T(8,128)S(1)} %get-tuple-element.71), channel_id=1, source_target_pairs={{0,3},{1,2},{2,1},{3,0},{4,7},{5,6},{6,5},{7,4},{8,11},{9,10},{10,... | collective-permute-start | bytes 73736 | tf_op jit(solution)/shard_map/ppermute | solution.py:429
  (7 other events, 9.8 us)
